TPU v7x, 128 devices: a whole 4x4x4 slice. The times are simulated.
128 devices in a mesh: rows: 16 (over z, x), dims: 8 (over y, core).
Axes of the slice: x: 4, y: 4, z: 4, core: 2. Of those that a mesh axis runs over, the one named last changes fastest.
Arguments:
- embeddings: bfloat16 [131072, 1024], P('rows', 'dims'), may hold values from -200 to 200
- sign_flips: int32 [1024], P('dims'), may hold values from -1 to 1, as said below
- row_order: int32 [131072], P('rows'), may hold values from 0 to 8191, as said below
- codebook: bfloat16 [64, 256, 16], replicated, may hold values from -4 to 4
Outputs:
- decoded: bfloat16 [131072, 1024], P(('rows', 'dims'))
- new_codebook: float32 [64, 256, 16], replicated
Inputs may be any that keep to these rules, and one draw needn't show every extreme that they name: `sign_flips`: each entry is -1 or 1. `row_order`: within each aligned block of 8192 entries the values are a permutation of 0 to 8191.
All inputs are finite; a program needn't handle non-finite values.
Results may differ from a plain program's by a relative error of at most 0.0065.
The roundings to bfloat16 on the way count: a program that leaves them out, or rounds other values in their place, can miss the bound.
Values may be sent and summed in bfloat16 or wider, within the bound.
A program may use at most 64 MiB of HBM per device.

v0:
```python
import math

import jax
import jax.numpy as jnp
from jax import lax
from jax.sharding import PartitionSpec as P

ANISO_GAIN = 1.0
SOFTNESS_LEVEL = 4.0
PRIOR_MASS = 1.0
STABILITY_FLOOR = 1e-06


def hadamard_table(order_size, number_type):
    row_ids = jnp.arange(order_size, dtype=jnp.int32)[:, None]
    column_numbers = jnp.arange(order_size, dtype=jnp.int32)[None, :]
    shared_offset = jnp.bitwise_and(row_ids, column_numbers)
    parity = jnp.zeros((order_size, order_size), jnp.int32)
    for shift_bits in range(max(order_size.bit_length() - 1, 0)):
        parity = parity + jnp.bitwise_and(jnp.right_shift(shared_offset, shift_bits), 1)
    return (1 - 2 * jnp.bitwise_and(parity, 1)).astype(number_type)


def rotate_local(signed_rows):
    row_count, full_width = signed_rows.shape
    inner_size = min(full_width, 128)
    outer_size = full_width // inner_size
    blocks = signed_rows.reshape(row_count, outer_size, inner_size)
    mixed_section = jnp.einsum(
        "rab,bc->rac",
        blocks,
        hadamard_table(inner_size, jnp.bfloat16),
        preferred_element_type=jnp.float32,
    )
    mixed_section = jnp.einsum(
        "rab,ca->rcb",
        mixed_section,
        hadamard_table(outer_size, jnp.float32),
        precision=lax.Precision.HIGHEST,
    )
    return (mixed_section.reshape(row_count, full_width) * (1.0 / math.sqrt(full_width))).astype(
        jnp.bfloat16
    )


def body(embeddings, sign_flips, row_order, codebook):
    rows_count = lax.axis_size("rows")
    dims_count = lax.axis_size("dims")
    devices = rows_count * dims_count
    block_rows, local_width = embeddings.shape
    row_dev = block_rows // dims_count
    piece_rows = block_rows // devices
    full_width = local_width * dims_count
    wide_input = embeddings.astype(jnp.float32)
    energy_total = lax.psum(jnp.sum(wide_input * wide_input), ("rows", "dims"))
    energy = energy_total / (row_dev * devices)
    signed = embeddings * sign_flips.astype(jnp.bfloat16)[None, :]
    outgoing = signed[row_order].reshape(devices, piece_rows, local_width)
    arrived = lax.all_to_all(outgoing, ("rows", "dims"), split_axis=0, concat_axis=0, tiled=True)
    whole_rows = (
        arrived.reshape(rows_count, dims_count, piece_rows, local_width)
        .transpose(0, 2, 1, 3)
        .reshape(row_dev, full_width)
    )
    regrouped = rotate_local(whole_rows)
    subspaces, codes, subspace_width = codebook.shape
    group_size = 8
    row_norms = jnp.sum(jnp.square(regrouped.astype(jnp.float32)), axis=1)
    stretch = ANISO_GAIN * subspaces * energy / (row_norms * row_norms + STABILITY_FLOOR)

    def one_group(group_index):
        columns = lax.dynamic_slice_in_dim(
            regrouped, group_index * (group_size * subspace_width), group_size * subspace_width, 1
        )
        columns = columns.reshape(row_dev, group_size, subspace_width)
        centres = lax.dynamic_slice_in_dim(codebook, group_index * group_size, group_size, 0)
        inner_products = jnp.einsum(
            "rgs,gks->grk", columns, centres, preferred_element_type=jnp.float32
        )
        wide_columns = columns.astype(jnp.float32)
        own_square = jnp.sum(wide_columns * wide_columns, axis=2).T[:, :, None]
        wide_centres = centres.astype(jnp.float32)
        centre_square = jnp.sum(wide_centres * wide_centres, axis=2)[:, None, :]
        parallel = own_square - inner_products
        squared_distance = (
            own_square
            - 2.0 * inner_products
            + centre_square
            + stretch[None, :, None] * parallel * parallel
        )
        assignment_scores = -squared_distance / SOFTNESS_LEVEL
        highest = jnp.max(assignment_scores, axis=2, keepdims=True)
        raised = jnp.exp(assignment_scores - highest)
        weights = (raised / jnp.sum(raised, axis=2, keepdims=True)).astype(jnp.bfloat16)
        decoded_part = jnp.einsum(
            "grk,gks->rgs", weights, centres, preferred_element_type=jnp.float32
        ).astype(jnp.bfloat16)
        weighted_sums = jnp.einsum(
            "grk,rgs->gks", weights, columns, preferred_element_type=jnp.float32
        )
        counts = jnp.sum(weights.astype(jnp.float32), axis=1)
        return (decoded_part.reshape(row_dev, group_size * subspace_width), weighted_sums, counts)

    decoded, weighted_sums, counts = lax.map(
        one_group, jnp.arange(subspaces // group_size, dtype=jnp.int32)
    )
    decoded = decoded.transpose(1, 0, 2).reshape(row_dev, full_width)
    weighted_sums = weighted_sums.reshape(subspaces, codes, subspace_width)
    counts = counts.reshape(subspaces, codes)
    total_sums, total_counts = lax.psum((weighted_sums, counts), ("rows", "dims"))
    new_codebook = (total_sums + PRIOR_MASS * codebook.astype(jnp.float32)) / (
        total_counts[:, :, None] + PRIOR_MASS
    )
    return (decoded, new_codebook)


def solution(mesh):
    return jax.shard_map(
        body,
        mesh=mesh,
        in_specs=(P("rows", "dims"), P("dims"), P("rows"), P()),
        out_specs=(P(("rows", "dims"), None), P()),
        check_vma=False,
    )
```

profile of v0, /device:TPU:1, one launch (start us, length us, event | category | flops | bytes accessed | tf_op | source)
XLA Modules:
  0.0 451.0 jit_solution(9500027417881602739)
XLA Ops:
  10.3 29.5 %gather_fusion = bf16[8192,128]{1,0:T(8,128)(2,1)} fusion(bf16[8192,128]{1,0:T(8,128)(2,1)S(1)} %broadcast_multiply_fusion, s32[8192]{0:T(1024)S(1)} %fusion.26), kind=kCustom, calls=%fused_computation | custom fusion | bytes 4227072 | tf_op jit(solution)/shard_map/gather | solution.py:58
  39.8 12.0 %all-to-all-start = ((bf16[128,64,128]{2,1,0:T(8,128)(2,1)}), bf16[128,64,128]{2,1,0:T(8,128)(2,1)}, u32[]{:S(2)}, u32[]{:S(2)}) async-start(bf16[128,64,128]{2,1,0:T(8,128)(2,1)} %bitcast.68), calls=%async_computation | async-start | bytes 4194304 | tf_op jit(solution)/shard_map/all_to_all | solution.py:59
  53.5 79.6 %psum.21 = f32[]{:T(128)} all-reduce(f32[]{:T(128)} %multiply_reduce_fusion.3), channel_id=1, replica_groups=mesh['rows'=16,'dims'=8] {'rows','dims'}, use_global_device_ids=true, to_apply=%region_1.0 | all-reduce | flops 1 | bytes 8 | tf_op jit(solution)/shard_map/psum | solution.py:55
  133.8 3.4 copy.16
  137.9 11.0 %multiply_reduce_fusion.2 = (f32[1024]{0:T(1024)S(1)}, bf16[1024,8,128]{2,1,0:T(8,128)(2,1)S(1)}) fusion(f32[1024,8,128]{2,1,0:T(8,128)S(1)} %fusion.24), kind=kOutput, calls=%fused_computation.28 | convolution fusion | flops 105905984 | bytes 6295552 | tf_op jit(solution)/shard_map/rab,ca->rcb/dot_general | solution.py:35
  151.8 143.4 %while.14 = (s32[]{:T(128)}, bf16[8,1024,128]{1,2,0:T(8,128)(2,1)}, f32[8,8,256,16]{2,3,1,0:T(8,128)}, f32[8,8,256]{2,1,0:T(8,128)}, s32[8]{0:T(128)S(1)}, /*ind...) while((s32[]{:T(128)}, bf16[8,1024,128]{1,2,0:T(8,128)(2,1)}, ...), condition=%wide.region_9.10_spmd, body=%wide.region_3.9_spmd.sunk | while | flops 233394432 | bytes 31700732 | solution.py:104
  155.2 6.7 %fusion.86 = (f32[8,1024]{1,0:T(8,128)S(1)}, f32[8,1024,256]{1,2,0:T(8,128)}) fusion(f32[1024]{0:T(1024)S(1)} %get-tuple-element.195, f32[8,256]{1,0:T(8,128)S(1)} %multiply_reduce_fusion.6, f32[8,1024]{1,0:T(8,128)S(1)} %bitcast.73, bf16[1024,8,16]{0,2,1:T(8,128)(2,1)S(1)} %bitcast.65, bf16[64,256,16]{1,2,0:T(8,128)(2,1)S(1)} %get-tuple-element.193, ...), kind=kOutput, calls=%fused_computation.77.clone.1 | convolution fusion | flops 90177792 | bytes 8794116 | tf_op jit(solution)/shard_map/while/body/eval_jaxpr/sub | solution.py:93
  161.9 4.2 convert_reduce_fusion.2
  173.1 6.7 %fusion.86 = (f32[8,1024]{1,0:T(8,128)S(1)}, f32[8,1024,256]{1,2,0:T(8,128)}) fusion(f32[1024]{0:T(1024)S(1)} %get-tuple-element.195, f32[8,256]{1,0:T(8,128)S(1)} %multiply_reduce_fusion.6, f32[8,1024]{1,0:T(8,128)S(1)} %bitcast.73, bf16[1024,8,16]{0,2,1:T(8,128)(2,1)S(1)} %bitcast.65, bf16[64,256,16]{1,2,0:T(8,128)(2,1)S(1)} %get-tuple-element.193, ...), kind=kOutput, calls=%fused_computation.77.clone.1 | convolution fusion | flops 90177792 | bytes 8794116 | tf_op jit(solution)/shard_map/while/body/eval_jaxpr/sub | solution.py:93
  179.8 4.2 convert_reduce_fusion.2
  191.0 6.7 %fusion.86 = (f32[8,1024]{1,0:T(8,128)S(1)}, f32[8,1024,256]{1,2,0:T(8,128)}) fusion(f32[1024]{0:T(1024)S(1)} %get-tuple-element.195, f32[8,256]{1,0:T(8,128)S(1)} %multiply_reduce_fusion.6, f32[8,1024]{1,0:T(8,128)S(1)} %bitcast.73, bf16[1024,8,16]{0,2,1:T(8,128)(2,1)S(1)} %bitcast.65, bf16[64,256,16]{1,2,0:T(8,128)(2,1)S(1)} %get-tuple-element.193, ...), kind=kOutput, calls=%fused_computation.77.clone.1 | convolution fusion | flops 90177792 | bytes 8794116 | tf_op jit(solution)/shard_map/while/body/eval_jaxpr/sub | solution.py:93
  197.7 4.2 convert_reduce_fusion.2
  208.9 6.7 %fusion.86 = (f32[8,1024]{1,0:T(8,128)S(1)}, f32[8,1024,256]{1,2,0:T(8,128)}) fusion(f32[1024]{0:T(1024)S(1)} %get-tuple-element.195, f32[8,256]{1,0:T(8,128)S(1)} %multiply_reduce_fusion.6, f32[8,1024]{1,0:T(8,128)S(1)} %bitcast.73, bf16[1024,8,16]{0,2,1:T(8,128)(2,1)S(1)} %bitcast.65, bf16[64,256,16]{1,2,0:T(8,128)(2,1)S(1)} %get-tuple-element.193, ...), kind=kOutput, calls=%fused_computation.77.clone.1 | convolution fusion | flops 90177792 | bytes 8794116 | tf_op jit(solution)/shard_map/while/body/eval_jaxpr/sub | solution.py:93
  215.6 4.2 convert_reduce_fusion.2
  226.8 6.7 %fusion.86 = (f32[8,1024]{1,0:T(8,128)S(1)}, f32[8,1024,256]{1,2,0:T(8,128)}) fusion(f32[1024]{0:T(1024)S(1)} %get-tuple-element.195, f32[8,256]{1,0:T(8,128)S(1)} %multiply_reduce_fusion.6, f32[8,1024]{1,0:T(8,128)S(1)} %bitcast.73, bf16[1024,8,16]{0,2,1:T(8,128)(2,1)S(1)} %bitcast.65, bf16[64,256,16]{1,2,0:T(8,128)(2,1)S(1)} %get-tuple-element.193, ...), kind=kOutput, calls=%fused_computation.77.clone.1 | convolution fusion | flops 90177792 | bytes 8794116 | tf_op jit(solution)/shard_map/while/body/eval_jaxpr/sub | solution.py:93
  233.5 4.2 convert_reduce_fusion.2
  244.7 6.7 %fusion.86 = (f32[8,1024]{1,0:T(8,128)S(1)}, f32[8,1024,256]{1,2,0:T(8,128)}) fusion(f32[1024]{0:T(1024)S(1)} %get-tuple-element.195, f32[8,256]{1,0:T(8,128)S(1)} %multiply_reduce_fusion.6, f32[8,1024]{1,0:T(8,128)S(1)} %bitcast.73, bf16[1024,8,16]{0,2,1:T(8,128)(2,1)S(1)} %bitcast.65, bf16[64,256,16]{1,2,0:T(8,128)(2,1)S(1)} %get-tuple-element.193, ...), kind=kOutput, calls=%fused_computation.77.clone.1 | convolution fusion | flops 90177792 | bytes 8794116 | tf_op jit(solution)/shard_map/while/body/eval_jaxpr/sub | solution.py:93
  251.4 4.2 convert_reduce_fusion.2
  262.6 6.7 %fusion.86 = (f32[8,1024]{1,0:T(8,128)S(1)}, f32[8,1024,256]{1,2,0:T(8,128)}) fusion(f32[1024]{0:T(1024)S(1)} %get-tuple-element.195, f32[8,256]{1,0:T(8,128)S(1)} %multiply_reduce_fusion.6, f32[8,1024]{1,0:T(8,128)S(1)} %bitcast.73, bf16[1024,8,16]{0,2,1:T(8,128)(2,1)S(1)} %bitcast.65, bf16[64,256,16]{1,2,0:T(8,128)(2,1)S(1)} %get-tuple-element.193, ...), kind=kOutput, calls=%fused_computation.77.clone.1 | convolution fusion | flops 90177792 | bytes 8794116 | tf_op jit(solution)/shard_map/while/body/eval_jaxpr/sub | solution.py:93
  269.3 4.2 convert_reduce_fusion.2
  280.5 6.7 %fusion.86 = (f32[8,1024]{1,0:T(8,128)S(1)}, f32[8,1024,256]{1,2,0:T(8,128)}) fusion(f32[1024]{0:T(1024)S(1)} %get-tuple-element.195, f32[8,256]{1,0:T(8,128)S(1)} %multiply_reduce_fusion.6, f32[8,1024]{1,0:T(8,128)S(1)} %bitcast.73, bf16[1024,8,16]{0,2,1:T(8,128)(2,1)S(1)} %bitcast.65, bf16[64,256,16]{1,2,0:T(8,128)(2,1)S(1)} %get-tuple-element.193, ...), kind=kOutput, calls=%fused_computation.77.clone.1 | convolution fusion | flops 90177792 | bytes 8794116 | tf_op jit(solution)/shard_map/while/body/eval_jaxpr/sub | solution.py:93
  287.2 4.2 convert_reduce_fusion.2
  295.3 3.9 copy.22
  299.2 141.7 %all-reduce.3.cloned.1.call-done = (f32[64,256,16]{1,2,0:T(8,128)}, f32[64,256]{1,0:T(8,128)}) async-done(((f32[64,256,16]{1,2,0:T(8,128)}, f32[64,256]{1,0:T(8,128)}), (f32[64,256,16]{1,2,0:T(8,128)}, f32[64,256]{1,0:T(8,128)})) %all-reduce.3.cloned.1.call-update) | async-done | bytes 1114128 | tf_op jit(solution)/shard_map/psum | solution.py:110
  (76 shorter events, 56.6 us)
Async XLA Ops:
  39.8 12.0 %copy-start = (bf16[8192,128]{1,0:T(8,128)(2,1)S(1)}, bf16[8192,128]{1,0:T(8,128)(2,1)}, u32[]{:S(2)}) copy-start(bf16[8192,128]{1,0:T(8,128)(2,1)} %param.6) | copy-start | bytes 6291460
  39.8 94.0 %all-to-all-start = ((bf16[128,64,128]{2,1,0:T(8,128)(2,1)}), bf16[128,64,128]{2,1,0:T(8,128)(2,1)}, u32[]{:S(2)}, u32[]{:S(2)}) async-start(bf16[128,64,128]{2,1,0:T(8,128)(2,1)} %bitcast.68), calls=%async_computation | async-start | bytes 4194304 | tf_op jit(solution)/shard_map/all_to_all | solution.py:59
  51.8 389.1 %all-reduce.3.cloned.1.call-start = ((), (), s32[]{:S(2)}) async-start(), calls=%async_computation.1 | async-start | bytes 2228224 | tf_op jit(solution)/shard_map/psum | solution.py:110
  137.9 13.9 %copy-start.1 = (bf16[64,256,16]{1,2,0:T(8,128)(2,1)S(1)}, bf16[64,256,16]{1,2,0:T(8,128)(2,1)}, u32[]{:S(2)}) copy-start(bf16[64,256,16]{1,2,0:T(8,128)(2,1)} %param.9) | copy-start | bytes 1572868
Sparse Core Ops, SparseCore 0:
  295.4 145.4 all-reduce.2
where the time goes:
time: 452 us; the launch traced here: 451 us
  waiting for transfers between devices  142 us (31%)
  matrix products  85.6 us (19%)
  blocking collectives  79.6 us (18%)
  local copies, waits for them, and re-layouts  55.7 us (12%)
  other arithmetic  50.2 us (11%)
  between operations  14.7 us (3%)
  starting transfers between devices  12 us (3%)
  loops' own time  11.5 us (3%)
    psum x1, waiting for transfers between devices, body(): lax.psum((weighted_sums, counts), ('rows', 'dims'))  142 us
    psum x1, blocking collectives, body(): energy_total = lax.psum(jnp.sum(wide_input * wide_input), ('rows', 'dims'))  79.6 us
    sub x8, matrix products, one_group(): raised = jnp.exp(assignment_scores - highest)  53.7 us
    reduce_sum x8, other arithmetic, one_group(): counts = jnp.sum(weights.astype(jnp.float32), axis=1)  33.4 us
    gather x1, local copies, waits for them, and re-layouts, body(): outgoing = signed[row_order].reshape(devices, piece_rows, local_width)  29.5 us
    dot_general x8, matrix products, one_group(): jnp.einsum('grk,rgs->gks', weights, columns, preferred_element_type=jnp.f...  14.8 us
    all_to_all x1, starting transfers between devices, body(): lax.all_to_all(outgoing, ('rows', 'dims'), split_axis=0, concat_axis=0, t...  12 us
    another operation x1, loops' own time, body(): lax.map(one_group, jnp.arange(subspaces // group_size, dtype=jnp.int32))  11.5 us
  transfers between devices with their start and end apart: 2, of which 1 were waited for; matrix products, arithmetic and copies ran while one was open for 1% of the time, Pallas kernels for 0%

commit v1 on v0

v1 whole, which is shorter than its diff:
```python
import math

import jax
import jax.numpy as jnp
from jax import lax
from jax.experimental import pallas as pl
from jax.experimental.pallas import tpu as pltpu
from jax.sharding import PartitionSpec as P

ANISO_GAIN = 1.0
SOFTNESS_LEVEL = 4.0
PRIOR_MASS = 1.0
STABILITY_FLOOR = 1e-06
LOG2E = math.log2(math.e)
NT = (((1,), (1,)), ((), ()))
F32 = jnp.float32
BF16 = jnp.bfloat16
LANES = 128


def hadamard(order):
    i = lax.broadcasted_iota(jnp.int32, (order, order), 0)
    j = lax.broadcasted_iota(jnp.int32, (order, order), 1)
    both = jnp.bitwise_and(i, j)
    parity = jnp.zeros((order, order), jnp.int32)
    for shift in range(order.bit_length() - 1):
        parity = parity + jnp.bitwise_and(jnp.right_shift(both, shift), 1)
    return (1 - 2 * jnp.bitwise_and(parity, 1)).astype(F32).astype(BF16)


def identity(order):
    i = lax.broadcasted_iota(jnp.int32, (order, order), 0)
    j = lax.broadcasted_iota(jnp.int32, (order, order), 1)
    return (i == j).astype(F32).astype(BF16)


def prepare_codes(m, ct_ref, c_ref, cb_ref, caug_ref):
    ct = ct_ref[m]
    width, codes = ct.shape
    wide = ct.astype(F32)
    c_ref[m] = wide.T.astype(BF16)
    square = jnp.sum(wide * wide, axis=0, keepdims=True) * (LOG2E / SOFTNESS_LEVEL)
    cb_ref[m] = jnp.broadcast_to(square, (LANES, codes)).T
    caug_ref[m, 0:width, :] = ct
    row = lax.broadcasted_iota(jnp.int32, (width, codes), 0)
    caug_ref[m, width : 2 * width, :] = jnp.where(row == 0, 1.0, 0.0).astype(BF16)


def rotate_block(block, rows, x_ref, rt_ref, own_ref, energy, width):
    outer = x_ref.shape[0]
    inner = x_ref.shape[2]
    h = hadamard(inner)
    parts = [
        lax.dot_general(h, x_ref[b, pl.ds(block * rows, rows), :], NT, preferred_element_type=F32)
        for b in range(outer)
    ]
    span = 1
    while span < outer:
        for b in range(outer):
            if not b & span:
                low, high = parts[b], parts[b | span]
                parts[b], parts[b | span] = low + high, low - high
        span *= 2
    scale = 1.0 / math.sqrt(outer * inner)
    total = jnp.zeros((1, rows), F32)
    for b in range(outer):
        rounded = (parts[b] * scale).astype(BF16)
        rt_ref[b * inner : (b + 1) * inner, :] = rounded
        wide = rounded.astype(F32)
        own = jnp.sum((wide * wide).reshape(inner // width, width, rows), axis=1)
        own_ref[b * (inner // width) : (b + 1) * (inner // width), :] = own
        total = total + jnp.sum(own, axis=0, keepdims=True)
    subspaces = outer * inner // width
    return ANISO_GAIN * subspaces * energy / (total * total + STABILITY_FLOOR)


def assign(m, rows, stretch, rt_ref, own_ref, c_ref, cb_ref, caug_ref, dt_ref, sums_ref, first):
    width = c_ref.shape[2]
    at = pl.ds(pl.multiple_of(m * width, width), width)
    x = rt_ref[at, :]
    own = own_ref[pl.ds(m, 1), :]
    g = jnp.dot(c_ref[m], x, preferred_element_type=F32)
    a = (1.0 + stretch * own) * (2.0 * LOG2E / SOFTNESS_LEVEL)
    b = stretch * (LOG2E / SOFTNESS_LEVEL)
    cb = cb_ref[m]
    t = g * (a - b * g) - jnp.concatenate([cb] * (rows // LANES), axis=1)
    e = jnp.exp2(t - jnp.max(t, axis=0, keepdims=True)).astype(BF16)
    o = jnp.dot(caug_ref[m], e, preferred_element_type=F32)
    inv = 1.0 / o[width : width + 1, :]
    dt_ref[at, :] = (o[0:width, :] * inv).astype(BF16)
    row = lax.broadcasted_iota(jnp.int32, (width, rows), 0)
    inv_high = inv.astype(BF16).astype(F32)
    tail = jnp.where(row == 0, inv_high, jnp.where(row == 1, inv - inv_high, 0.0))
    left = jnp.concatenate([x.astype(F32) * inv, tail], axis=0).astype(BF16)
    s = lax.dot_general(left, e, NT, preferred_element_type=F32)
    s = jnp.concatenate([s[0:width], s[width : width + 1] + s[width + 1 : width + 2], s[width + 1 : width + 8]], axis=0)

    sums_ref[m] = jnp.where(first, 0.0, sums_ref[m]) + s


def compute_kernel(energy_ref, x_ref, ct_ref, out_ref, sums_ref, c_ref, cb_ref, caug_ref, rt_ref, own_ref, dt_ref):
    subspaces, width, codes = ct_ref.shape
    outer, all_rows, inner = x_ref.shape
    rows = rt_ref.shape[1]
    energy = energy_ref[0, 0]

    def prep(m, carry):
        prepare_codes(m, ct_ref, c_ref, cb_ref, caug_ref)
        return carry

    lax.fori_loop(0, subspaces, prep, 0)

    def one_block(block, carry):
        stretch = rotate_block(block, rows, x_ref, rt_ref, own_ref, energy, width)

        def one(i, carry):
            for k in range(UNROLL):
                assign(
                    i * UNROLL + k, rows, stretch, rt_ref, own_ref, c_ref, cb_ref, caug_ref, dt_ref, sums_ref, block == 0
                )
            return carry

        lax.fori_loop(0, subspaces // UNROLL, one, 0)
        eye = identity(rows)
        for b in range(outer):
            flipped = lax.dot_general(eye, dt_ref[b * inner : (b + 1) * inner, :], NT, preferred_element_type=F32)
            out_ref[pl.ds(pl.multiple_of(block * rows, rows), rows), b * inner : (b + 1) * inner] = flipped.astype(BF16)
        return carry

    lax.fori_loop(0, all_rows // rows, one_block, 0)


UNROLL = 2


def compute(energy, x, ct):
    subspaces, width, codes = ct.shape
    outer, all_rows, inner = x.shape
    rows = 256
    vmem = pl.BlockSpec(memory_space=pltpu.VMEM)
    return pl.pallas_call(
        compute_kernel,
        out_shape=(
            jax.ShapeDtypeStruct((all_rows, outer * inner), BF16),
            jax.ShapeDtypeStruct((subspaces, width + 8, codes), F32),
        ),
        in_specs=[pl.BlockSpec(memory_space=pltpu.SMEM), vmem, vmem],
        out_specs=(vmem, vmem),
        scratch_shapes=[
            pltpu.VMEM((subspaces, codes, width), BF16),
            pltpu.VMEM((subspaces, codes, LANES), F32),
            pltpu.VMEM((subspaces, 2 * width, codes), BF16),
            pltpu.VMEM((outer * inner, rows), BF16),
            pltpu.VMEM((subspaces, rows), F32),
            pltpu.VMEM((outer * inner, rows), BF16),
        ],
        compiler_params=pltpu.CompilerParams(vmem_limit_bytes=48 * 1024 * 1024),
        name="assign_codes",
    )(energy, x, ct)


def body(embeddings, sign_flips, row_order, codebook):
    rows_count = lax.axis_size("rows")
    dims_count = lax.axis_size("dims")
    devices = rows_count * dims_count
    block_rows, local_width = embeddings.shape
    row_dev = block_rows // dims_count
    piece_rows = block_rows // devices
    wide_input = embeddings.astype(F32)
    energy_total = lax.psum(jnp.sum(wide_input * wide_input), ("rows", "dims"))
    energy = energy_total / (row_dev * devices)
    signed = embeddings * sign_flips.astype(BF16)[None, :]
    outgoing = signed[row_order].reshape(devices, piece_rows, local_width)
    arrived = lax.all_to_all(outgoing, ("rows", "dims"), split_axis=0, concat_axis=0, tiled=True)
    x = (
        arrived.reshape(rows_count, dims_count, piece_rows, local_width)
        .transpose(1, 0, 2, 3)
        .reshape(dims_count, row_dev, local_width)
    )
    ct = codebook.transpose(0, 2, 1)
    width = ct.shape[1]
    decoded, sums = compute(energy.reshape(1, 1), x, ct)
    sums = lax.psum(sums[:, : width + 1], ("rows", "dims"))
    new = (sums[:, :width] + PRIOR_MASS * ct.astype(F32)) / (sums[:, width : width + 1] + PRIOR_MASS)
    return decoded, new.transpose(0, 2, 1)


def solution(mesh):
    return jax.shard_map(
        body,
        mesh=mesh,
        in_specs=(P("rows", "dims"), P("dims"), P("rows"), P()),
        out_specs=(P(("rows", "dims"), None), P()),
        check_vma=False,
    )
```

time: 452 us -> 406 us (0.90)
  Pallas kernels: 0 us -> 113 us
  matrix products: 85.6 us -> 0 us
  other arithmetic: 50.2 us -> 8.32 us
  local copies, waits for them, and re-layouts: 55.7 us -> 31.4 us
  loops' own time: 11.5 us -> 0 us
  waiting for transfers between devices: 142 us -> 147 us
    pallas_call x0 -> x1, Pallas kernels: none -> 113 us  [compute(): pl.pallas_call(compute_kernel, out_shape=(jax.ShapeDtypeStruct((all_rows,...]
    sub x8 -> x0, matrix products: 53.7 us -> none  [one_group(): raised = jnp.exp(assignment_scores - highest)]
    reduce_sum x24 -> x0, other arithmetic: 42.2 us -> none  [the longest x8 33.4 us: one_group(): counts = jnp.sum(weights.astype(jnp.float32), axis=1)]
    dot_general x18 -> x0, matrix products: 31.9 us -> none  [the longest x8 14.8 us: one_group(): jnp.einsum('grk,rgs->gks', weights, columns, preferred_element_type=jnp.f...]
    another operation x1 -> x0, loops' own time: 11.5 us -> none  [body(): lax.map(one_group, jnp.arange(subspaces // group_size, dtype=jnp.int32))]
    dynamic_update_slice x16 -> x0, local copies, waits for them, and re-layouts: 10.7 us -> none  [body(): lax.map(one_group, jnp.arange(subspaces // group_size, dtype=jnp.int32))]
    dynamic_slice x8 -> x0, local copies, waits for them, and re-layouts: 5.3 us -> none  [body(): lax.map(one_group, jnp.arange(subspaces // group_size, dtype=jnp.int32))]
    psum x1, waiting for transfers between devices: 142 us -> 147 us  [body(): sums = lax.psum(sums[:, :width + 1], ('rows', 'dims'))]
  transfers between devices with their start and end apart: 2 -> 2, of which waited for: 1 -> 1; matrix products, arithmetic and copies ran while one was open for 1% -> 0% of each run, Pallas kernels for 0% -> 0%
where the time goes in v1:
time: 406 us
  waiting for transfers between devices  147 us (36%)
  Pallas kernels  113 us (28%)
  blocking collectives  79.6 us (20%)
  local copies, waits for them, and re-layouts  31.4 us (8%)
  between operations  14.7 us (4%)
  starting transfers between devices  12 us (3%)
  other arithmetic  8.32 us (2%)
    psum x1, waiting for transfers between devices, body(): sums = lax.psum(sums[:, :width + 1], ('rows', 'dims'))  147 us
    pallas_call x1, Pallas kernels, compute(): pl.pallas_call(compute_kernel, out_shape=(jax.ShapeDtypeStruct((all_rows,...  113 us
    psum x1, blocking collectives, body(): energy_total = lax.psum(jnp.sum(wide_input * wide_input), ('rows', 'dims'))  79.6 us
    gather x1, local copies, waits for them, and re-layouts, body(): outgoing = signed[row_order].reshape(devices, piece_rows, local_width)  29.5 us
    all_to_all x1, starting transfers between devices, body(): lax.all_to_all(outgoing, ('rows', 'dims'), split_axis=0, concat_axis=0, t...  12 us
  transfers between devices with their start and end apart: 2, of which 1 were waited for; matrix products, arithmetic and copies ran while one was open for 0% of the time, Pallas kernels for 0%

profile of v1, /device:TPU:1, one launch (start us, length us, event | category | flops | bytes accessed | tf_op | source)
XLA Modules:
  0.0 405.5 jit_solution(10084363212693888874)
XLA Ops:
  7.2 0.7 convert_element_type.10
  7.8 0.8 fusion.2
  8.6 1.7 broadcast_multiply_fusion
  10.3 29.5 %gather_fusion = bf16[8192,128]{1,0:T(8,128)(2,1)} fusion(bf16[8192,128]{1,0:T(8,128)(2,1)S(1)} %broadcast_multiply_fusion, s32[8192]{0:T(1024)S(1)} %fusion.2), kind=kCustom, calls=%fused_computation | custom fusion | bytes 4227072 | tf_op jit(solution)/shard_map/gather | solution.py:173
  39.8 0.0 copy-start.1
  39.8 12.0 %all-to-all-start = ((bf16[128,64,128]{2,1,0:T(8,128)(2,1)}), bf16[128,64,128]{2,1,0:T(8,128)(2,1)}, u32[]{:S(2)}, u32[]{:S(2)}) async-start(bf16[128,64,128]{2,1,0:T(8,128)(2,1)} %bitcast.16), calls=%async_computation | async-start | bytes 4194304 | tf_op jit(solution)/shard_map/all_to_all | solution.py:174
  51.8 0.0 all-reduce.2.cloned.1.call-start
  51.8 0.0 copy-done.1
  51.8 1.7 multiply_reduce_fusion
  53.5 79.6 %psum.14 = f32[]{:T(128)} all-reduce(f32[]{:T(128)} %multiply_reduce_fusion), channel_id=1, replica_groups=mesh['rows'=16,'dims'=8] {'rows','dims'}, use_global_device_ids=true, to_apply=%region_1.0 | all-reduce | flops 1 | bytes 8 | tf_op jit(solution)/shard_map/psum | solution.py:170
  133.8 0.0 all-to-all-done
  133.8 0.0 copy-start
  133.8 1.9 copy.6
  135.7 0.0 copy-done
  135.7 112.8 %assign_codes.1 = (bf16[1024,1024]{1,0:T(8,128)(2,1)}, f32[64,24,256]{2,1,0:T(8,128)}) custom-call(f32[1,1]{1,0:T(1,128)} %bitcast.energy_ref, bf16[8,1024,128]{2,1,0:T(8,128)(2,1)S(1)} %bitcast.14, bf16[64,16,256]{2,1,0:T(8,128)(2,1)S(1)} %bitcast.15), custom_call_target="tpu_custom_call" | custom-call | tf_op jit(solution)/shard_map/assign_codes/pallas_call | solution.py:141
  248.5 0.0 all-reduce.2.cloned.1.call-update
  248.6 146.6 %all-reduce.2.cloned.1.call-done = f32[64,17,256]{2,1,0:T(8,128)} async-done(((f32[64,17,256]{2,1,0:T(8,128)}), f32[64,17,256]{2,1,0:T(8,128)}) %all-reduce.2.cloned.1.call-update) | async-done | bytes 1114128 | tf_op jit(solution)/shard_map/psum | solution.py:183
  395.2 1.1 slice_add_fusion.1
  396.3 2.4 fusion.1
  (1 shorter events, 0.0 us)
Async XLA Ops:
  39.8 12.0 %copy-start.1 = (bf16[8192,128]{1,0:T(8,128)(2,1)S(1)}, bf16[8192,128]{1,0:T(8,128)(2,1)}, u32[]{:S(2)}) copy-start(bf16[8192,128]{1,0:T(8,128)(2,1)} %param.4) | copy-start | bytes 6291460
  39.8 94.0 %all-to-all-start = ((bf16[128,64,128]{2,1,0:T(8,128)(2,1)}), bf16[128,64,128]{2,1,0:T(8,128)(2,1)}, u32[]{:S(2)}, u32[]{:S(2)}) async-start(bf16[128,64,128]{2,1,0:T(8,128)(2,1)} %bitcast.16), calls=%async_computation | async-start | bytes 4194304 | tf_op jit(solution)/shard_map/all_to_all | solution.py:174
  51.8 343.4 %all-reduce.2.cloned.1.call-start = ((), (), s32[]{:S(2)}) async-start(), calls=%async_computation.1 | async-start | bytes 3145728 | tf_op jit(solution)/shard_map/psum | solution.py:183
  133.8 1.9 copy-start
Sparse Core Ops, SparseCore 0:
  248.7 146.4 all-reduce.1

commit v2 on v1

--- a/solution.py
+++ b/solution.py
@@ -74,28 +74,32 @@
     return ANISO_GAIN * subspaces * energy / (total * total + STABILITY_FLOOR)
 
 
-def assign(m, rows, stretch, rt_ref, own_ref, c_ref, cb_ref, caug_ref, dt_ref, sums_ref, first):
+def assign(ms, rows, stretch, rt_ref, own_ref, c_ref, cb_ref, caug_ref, dt_ref, sums_ref, first):
     width = c_ref.shape[2]
-    at = pl.ds(pl.multiple_of(m * width, width), width)
-    x = rt_ref[at, :]
-    own = own_ref[pl.ds(m, 1), :]
-    g = jnp.dot(c_ref[m], x, preferred_element_type=F32)
-    a = (1.0 + stretch * own) * (2.0 * LOG2E / SOFTNESS_LEVEL)
+    ats = [pl.ds(pl.multiple_of(m * width, width), width) for m in ms]
+    xs = [rt_ref[at, :] for at in ats]
+    gs = [jnp.dot(c_ref[m], x, preferred_element_type=F32) for m, x in zip(ms, xs)]
     b = stretch * (LOG2E / SOFTNESS_LEVEL)
-    cb = cb_ref[m]
-    t = g * (a - b * g) - jnp.concatenate([cb] * (rows // LANES), axis=1)
-    e = jnp.exp2(t - jnp.max(t, axis=0, keepdims=True)).astype(BF16)
-    o = jnp.dot(caug_ref[m], e, preferred_element_type=F32)
-    inv = 1.0 / o[width : width + 1, :]
-    dt_ref[at, :] = (o[0:width, :] * inv).astype(BF16)
+    es = []
+    for m, g in zip(ms, gs):
+        a = (1.0 + stretch * own_ref[pl.ds(m, 1), :]) * (2.0 * LOG2E / SOFTNESS_LEVEL)
+        t = g * (a - b * g) - jnp.concatenate([cb_ref[m]] * (rows // LANES), axis=1)
+        es.append(jnp.exp2(t - jnp.max(t, axis=0, keepdims=True)).astype(BF16))
+    os = [jnp.dot(caug_ref[m], e, preferred_element_type=F32) for m, e in zip(ms, es)]
     row = lax.broadcasted_iota(jnp.int32, (width, rows), 0)
-    inv_high = inv.astype(BF16).astype(F32)
-    tail = jnp.where(row == 0, inv_high, jnp.where(row == 1, inv - inv_high, 0.0))
-    left = jnp.concatenate([x.astype(F32) * inv, tail], axis=0).astype(BF16)
-    s = lax.dot_general(left, e, NT, preferred_element_type=F32)
-    s = jnp.concatenate([s[0:width], s[width : width + 1] + s[width + 1 : width + 2], s[width + 1 : width + 8]], axis=0)
-
-    sums_ref[m] = jnp.where(first, 0.0, sums_ref[m]) + s
+    lefts = []
+    for at, o, x in zip(ats, os, xs):
+        inv = 1.0 / o[width : width + 1, :]
+        dt_ref[at, :] = (o[0:width, :] * inv).astype(BF16)
+        inv_high = inv.astype(BF16).astype(F32)
+        tail = jnp.where(row == 0, inv_high, jnp.where(row == 1, inv - inv_high, 0.0))
+        lefts.append(jnp.concatenate([x.astype(F32) * inv, tail], axis=0).astype(BF16))
+    ss = [lax.dot_general(left, e, NT, preferred_element_type=F32) for left, e in zip(lefts, es)]
+    for m, s in zip(ms, ss):
+        s = jnp.concatenate(
+            [s[0:width], s[width : width + 1] + s[width + 1 : width + 2], s[width + 1 : width + 8]], axis=0
+        )
+        sums_ref[m] = jnp.where(first, 0.0, sums_ref[m]) + s
 
 
 def compute_kernel(energy_ref, x_ref, ct_ref, out_ref, sums_ref, c_ref, cb_ref, caug_ref, rt_ref, own_ref, dt_ref):
@@ -114,10 +118,8 @@
         stretch = rotate_block(block, rows, x_ref, rt_ref, own_ref, energy, width)
 
         def one(i, carry):
-            for k in range(UNROLL):
-                assign(
-                    i * UNROLL + k, rows, stretch, rt_ref, own_ref, c_ref, cb_ref, caug_ref, dt_ref, sums_ref, block == 0
-                )
+            ms = [i * UNROLL + k for k in range(UNROLL)]
+            assign(ms, rows, stretch, rt_ref, own_ref, c_ref, cb_ref, caug_ref, dt_ref, sums_ref, block == 0)
             return carry
 
         lax.fori_loop(0, subspaces // UNROLL, one, 0)
@@ -130,7 +132,7 @@
     lax.fori_loop(0, all_rows // rows, one_block, 0)
 
 
-UNROLL = 2
+UNROLL = 8
 
 
 def compute(energy, x, ct):
@@ -159,30 +161,265 @@
     )(energy, x, ct)
 
 
+MESH = pl.DeviceIdType.MESH
+
+
+def wait_bytes(ref, sem):
+    pltpu.make_async_copy(ref, ref, sem).wait()
+
+
+def regroup_kernel(
+    emb_ref, sign_ref, order_ref, x_ref, energy_ref,
+    wide, stage, send, part, part_rows, got_dims, got_rows,
+    send_sem, recv_sem, esend_dims, erecv_dims, esend_rows, erecv_rows,
+):
+    r, d = lax.axis_index("rows"), lax.axis_index("dims")
+    n_rows, n_dims = lax.axis_size("rows"), lax.axis_size("dims")
+    devices, piece, inner = send.shape
+    block = emb_ref.shape[0]
+
+    barrier = pltpu.get_barrier_semaphore()
+
+    def greet(i, carry):
+        step = i + 1
+        there = lax.rem(r * n_dims + d + step, devices)
+        pl.semaphore_signal(barrier, inc=1, device_id=(there // n_dims, lax.rem(there, n_dims)), device_id_type=MESH)
+        return carry
+
+    lax.fori_loop(0, devices - 1, greet, 0)
+
+    sign = sign_ref[...].astype(F32)
+    chunk = 256
+
+    def widen(i, acc):
+        at = pl.ds(pl.multiple_of(i * chunk, chunk), chunk)
+        v = emb_ref[at, :].astype(F32)
+        wide[at, :] = v * sign
+        return acc + jnp.sum((v * v).reshape(chunk // 8, 8, inner), axis=0)
+
+    part[...] = lax.fori_loop(0, block // chunk, widen, jnp.zeros((8, inner), F32))
+    pl.semaphore_wait(barrier, devices - 1)
+
+    def energy_copy(axis, src, dst, there, send_s, recv_s):
+        return pltpu.make_async_remote_copy(
+            src_ref=src, dst_ref=dst, send_sem=send_s, recv_sem=recv_s, device_id=there, device_id_type=MESH
+        )
+
+    for k in range(1, n_dims):
+        there = lax.rem(d + k, n_dims)
+        energy_copy(1, part, got_dims.at[k], (r, there), esend_dims.at[k], erecv_dims.at[k]).start()
+
+    def gather(j, k, slot):
+        to_r, to_d = lax.rem(r + j, n_rows), lax.rem(d + k, n_dims)
+        q = to_r * n_dims + to_d
+        first = q * piece
+        for u in range(piece):
+            stage[slot, pl.ds(u, 1), :] = wide[pl.ds(order_ref[first + u], 1), :]
+        send[q] = stage[slot].astype(BF16)
+        here = x_ref.at[d, pl.ds(pl.multiple_of(r * piece, piece), piece), :]
+        return q, here, to_r, to_d
+
+    def one_piece(j, k, slot):
+        q, here, to_r, to_d = gather(j, k, slot)
+        pltpu.make_async_remote_copy(
+            src_ref=send.at[q], dst_ref=here, send_sem=send_sem.at[j], recv_sem=recv_sem.at[j],
+            device_id=(to_r, to_d), device_id_type=MESH,
+        ).start()
+
+    def group(j, carry):
+        def pair(i, carry):
+            for slot in range(2):
+                one_piece(j, i * 2 + slot, slot)
+            return carry
+
+        lax.fori_loop(0, n_dims // 2, pair, 0)
+        return carry
+
+    q, here = gather(0, 0, 0)[:2]
+    pltpu.make_async_copy(send.at[q], here, recv_sem.at[0]).start()
+    for k in range(1, n_dims):
+        one_piece(0, k, k % 2)
+    lax.fori_loop(1, n_rows // 4, group, 0)
+
+    total = part[...]
+    for k in range(1, n_dims):
+        wait_bytes(part, erecv_dims.at[k])
+        total = total + got_dims[k]
+    part_rows[...] = total
+    for k in range(1, n_rows):
+        there = lax.rem(r + k, n_rows)
+        energy_copy(0, part_rows, got_rows.at[k], (there, d), esend_rows.at[k], erecv_rows.at[k]).start()
+    lax.fori_loop(n_rows // 4, n_rows, group, 0)
+    for k in range(1, n_rows):
+        wait_bytes(part, erecv_rows.at[k])
+        total = total + got_rows[k]
+    energy_ref[...] = jnp.broadcast_to(jnp.sum(total, keepdims=True), energy_ref.shape) / (block * n_rows)
+
+    wait_bytes(send.at[pl.ds(0, n_dims - 1)], send_sem.at[0])
+    for j in range(n_rows):
+        if j:
+            wait_bytes(send.at[pl.ds(0, n_dims)], send_sem.at[j])
+        at = pl.ds(pl.multiple_of(lax.rem(r + n_rows - j, n_rows) * piece, piece), piece)
+        wait_bytes(x_ref.at[:, at, :], recv_sem.at[j])
+    for k in range(1, n_dims):
+        wait_bytes(part, esend_dims.at[k])
+    for k in range(1, n_rows):
+        wait_bytes(part, esend_rows.at[k])
+
+
+def regroup(embeddings, sign_flips, row_order):
+    n_rows, n_dims = lax.axis_size("rows"), lax.axis_size("dims")
+    block, inner = embeddings.shape
+    devices = n_rows * n_dims
+    piece = block // devices
+    vmem = pl.BlockSpec(memory_space=pltpu.VMEM)
+    dma = pltpu.SemaphoreType.DMA
+    return pl.pallas_call(
+        regroup_kernel,
+        out_shape=(
+            jax.ShapeDtypeStruct((n_dims, block // n_dims, inner), BF16),
+            jax.ShapeDtypeStruct((8, inner), F32),
+        ),
+        in_specs=[vmem, vmem, pl.BlockSpec(memory_space=pltpu.SMEM)],
+        out_specs=(vmem, vmem),
+        scratch_shapes=[
+            pltpu.VMEM((block, inner), F32),
+            pltpu.VMEM((2, piece, inner), F32),
+            pltpu.VMEM((devices, piece, inner), BF16),
+            pltpu.VMEM((8, inner), F32),
+            pltpu.VMEM((8, inner), F32),
+            pltpu.VMEM((n_dims, 8, inner), F32),
+            pltpu.VMEM((n_rows, 8, inner), F32),
+            dma((n_rows,)),
+            dma((n_rows,)),
+            dma((n_dims,)),
+            dma((n_dims,)),
+            dma((n_rows,)),
+            dma((n_rows,)),
+        ],
+        compiler_params=pltpu.CompilerParams(
+            collective_id=0, has_side_effects=True, vmem_limit_bytes=32 * 1024 * 1024
+        ),
+        name="regroup_rows",
+    )(embeddings, sign_flips.reshape(1, inner), row_order)
+
+
+def combine_kernel(
+    sums_ref, ct_ref, out_ref, low, counts, got_low, got_counts, both, got_both,
+    sem_a, sem_b, sem_c, sem_d, sem_e, sem_f, sem_g, sem_h, sem_i, sem_j,
+):
+    r, d = lax.axis_index("rows"), lax.axis_index("dims")
+    n_rows, n_dims = lax.axis_size("rows"), lax.axis_size("dims")
+    subspaces, width, codes = ct_ref.shape
+    group = subspaces // n_dims
+    half = codes * group // n_rows
+
+    barrier = pltpu.get_barrier_semaphore()
+    for k in range(1, n_dims):
+        pl.semaphore_signal(barrier, inc=1, device_id=(r, lax.rem(d + k, n_dims)), device_id_type=MESH)
+    for k in range(1, n_rows):
+        pl.semaphore_signal(barrier, inc=1, device_id=(lax.rem(r + k, n_rows), d), device_id_type=MESH)
+
+    for s in range(subspaces):
+        low[s] = sums_ref[s, 0:width, :].astype(BF16)
+        counts[s : s + 1, :] = sums_ref[s, width : width + 1, :]
+    pl.semaphore_wait(barrier, n_dims + n_rows - 2)
+
+    def remote(src, dst, there, send_s, recv_s):
+        return pltpu.make_async_remote_copy(
+            src_ref=src, dst_ref=dst, send_sem=send_s, recv_sem=recv_s, device_id=there, device_id_type=MESH
+        )
+
+    sent = []
+
+    def go(*args):
+        copy = remote(*args)
+        copy.start()
+        sent.append(copy)
+
+    for k in range(1, n_dims):
+        there = lax.rem(d + k, n_dims)
+        at = pl.ds(pl.multiple_of(there * group, group), group)
+        go(low.at[at], got_low.at[k], (r, there), sem_a.at[k], sem_b.at[k])
+        go(counts.at[at], got_counts.at[k], (r, there), sem_c.at[k], sem_d.at[k])
+    mine = pl.ds(pl.multiple_of(d * group, group), group)
+    total = sums_ref[mine, 0:width, :]
+    total_counts = counts[mine, :]
+    for k in range(1, n_dims):
+        wait_bytes(got_low.at[k], sem_b.at[k])
+        wait_bytes(got_counts.at[k], sem_d.at[k])
+        total = total + got_low[k].astype(F32)
+        total_counts = total_counts + got_counts[k]
+    for s in range(group):
+        for h in range(codes // half):
+            lanes = slice(h * half, (h + 1) * half)
+            both[s * (codes // half) + h, 0:width, :] = total[s, :, lanes]
+            both[s * (codes // half) + h, width : width + 8, :] = jnp.broadcast_to(total_counts[s : s + 1, lanes], (8, half))
+    for k in range(1, n_rows):
+        there = lax.rem(r + k, n_rows)
+        go(both.at[there], got_both.at[k], (there, d), sem_e.at[k], sem_f.at[k])
+    total = both[r]
+    for k in range(1, n_rows):
+        wait_bytes(got_both.at[k], sem_f.at[k])
+        total = total + got_both[k]
+
+    def place(rank):
+        return d * group + rank // (codes // half), pl.ds(pl.multiple_of(lax.rem(rank, codes // half) * half, half), half)
+
+    s, lanes = place(r)
+    out_ref[s, :, lanes] = (total[0:width] + PRIOR_MASS * ct_ref[s, :, lanes].astype(F32)) / (
+        total[width : width + 1] + PRIOR_MASS
+    )
+    for k in range(1, n_rows):
+        there = lax.rem(r + k, n_rows)
+        go(out_ref.at[s, :, lanes], out_ref.at[s, :, lanes], (there, d), sem_g.at[k], sem_h.at[k])
+    for k in range(1, n_rows):
+        s, lanes = place(lax.rem(r + n_rows - k, n_rows))
+        wait_bytes(out_ref.at[s, :, lanes], sem_h.at[k])
+    for k in range(1, n_dims):
+        go(out_ref.at[mine], out_ref.at[mine], (r, lax.rem(d + k, n_dims)), sem_i.at[k], sem_j.at[k])
+    for k in range(1, n_dims):
+        there = lax.rem(d + n_dims - k, n_dims)
+        wait_bytes(out_ref.at[pl.ds(pl.multiple_of(there * group, group), group)], sem_j.at[k])
+    for copy in sent:
+        copy.wait_send()
+
+
+def combine(sums, ct):
+    n_rows, n_dims = lax.axis_size("rows"), lax.axis_size("dims")
+    subspaces, width, codes = ct.shape
+    group = subspaces // n_dims
+    half = codes * group // n_rows
+    vmem = pl.BlockSpec(memory_space=pltpu.VMEM)
+    dma = pltpu.SemaphoreType.DMA
+    return pl.pallas_call(
+        combine_kernel,
+        out_shape=jax.ShapeDtypeStruct((subspaces, width, codes), F32),
+        in_specs=[vmem, vmem],
+        out_specs=vmem,
+        scratch_shapes=[
+            pltpu.VMEM((subspaces, width, codes), BF16),
+            pltpu.VMEM((subspaces, codes), F32),
+            pltpu.VMEM((n_dims, group, width, codes), BF16),
+            pltpu.VMEM((n_dims, group, codes), F32),
+            pltpu.VMEM((n_rows, width + 8, half), F32),
+            pltpu.VMEM((n_rows, width + 8, half), F32),
+        ]
+        + [dma((n_dims,))] * 4
+        + [dma((n_rows,))] * 4
+        + [dma((n_dims,))] * 2,
+        compiler_params=pltpu.CompilerParams(
+            collective_id=1, has_side_effects=True, vmem_limit_bytes=32 * 1024 * 1024
+        ),
+        name="combine_sums",
+    )(sums, ct)
+
+
 def body(embeddings, sign_flips, row_order, codebook):
-    rows_count = lax.axis_size("rows")
-    dims_count = lax.axis_size("dims")
-    devices = rows_count * dims_count
-    block_rows, local_width = embeddings.shape
-    row_dev = block_rows // dims_count
-    piece_rows = block_rows // devices
-    wide_input = embeddings.astype(F32)
-    energy_total = lax.psum(jnp.sum(wide_input * wide_input), ("rows", "dims"))
-    energy = energy_total / (row_dev * devices)
-    signed = embeddings * sign_flips.astype(BF16)[None, :]
-    outgoing = signed[row_order].reshape(devices, piece_rows, local_width)
-    arrived = lax.all_to_all(outgoing, ("rows", "dims"), split_axis=0, concat_axis=0, tiled=True)
-    x = (
-        arrived.reshape(rows_count, dims_count, piece_rows, local_width)
-        .transpose(1, 0, 2, 3)
-        .reshape(dims_count, row_dev, local_width)
-    )
     ct = codebook.transpose(0, 2, 1)
-    width = ct.shape[1]
-    decoded, sums = compute(energy.reshape(1, 1), x, ct)
-    sums = lax.psum(sums[:, : width + 1], ("rows", "dims"))
-    new = (sums[:, :width] + PRIOR_MASS * ct.astype(F32)) / (sums[:, width : width + 1] + PRIOR_MASS)
-    return decoded, new.transpose(0, 2, 1)
+    x, energy = regroup(embeddings, sign_flips, row_order)
+    decoded, sums = compute(energy, x, ct)
+    return decoded, combine(sums, ct).transpose(0, 2, 1)
 
 
 def solution(mesh):

time: 406 us -> 144 us (0.35)
  waiting for transfers between devices: 147 us -> 0 us
  blocking collectives: 79.6 us -> 0 us
  local copies, waits for them, and re-layouts: 31.4 us -> 3.97 us
  Pallas kernels: 113 us -> 139 us
  between operations: 14.7 us -> 0.67 us
  starting transfers between devices: 12 us -> 0 us
  other arithmetic: 8.32 us -> 0 us
    psum x1 -> x0, waiting for transfers between devices: 147 us -> none  [body(): sums = lax.psum(sums[:, :width + 1], ('rows', 'dims'))]
    pallas_call x0 -> x2, Pallas kernels: none -> 84 us  [the longest x1 47.7 us: regroup(): pl.pallas_call(regroup_kernel, out_shape=(jax.ShapeDtypeStruct((n_dims, b...]
    psum x1 -> x0, blocking collectives: 79.6 us -> none  [body(): energy_total = lax.psum(jnp.sum(wide_input * wide_input), ('rows', 'dims'))]
    pallas_call x1, Pallas kernels: 113 us -> 55.4 us  [compute(): pl.pallas_call(compute_kernel, out_shape=(jax.ShapeDtypeStruct((all_rows,...]
    gather x1 -> x0, local copies, waits for them, and re-layouts: 29.5 us -> none  [body(): outgoing = signed[row_order].reshape(devices, piece_rows, local_width)]
    all_to_all x1 -> x0, starting transfers between devices: 12 us -> none  [body(): lax.all_to_all(outgoing, ('rows', 'dims'), split_axis=0, concat_axis=0, t...]
  transfers between devices with their start and end apart: 2 -> 0, of which waited for: 1 -> 0; matrix products, arithmetic and copies ran while one was open for 0% -> 0% of each run, Pallas kernels for 0% -> 0%
where the time goes in v2:
time: 144 us
  Pallas kernels  139 us (97%)
  local copies, waits for them, and re-layouts  3.97 us (3%)
    pallas_call x1, Pallas kernels, compute(): pl.pallas_call(compute_kernel, out_shape=(jax.ShapeDtypeStruct((all_rows,...  55.4 us
    pallas_call x1, Pallas kernels, regroup(): pl.pallas_call(regroup_kernel, out_shape=(jax.ShapeDtypeStruct((n_dims, b...  47.7 us
    pallas_call x1, Pallas kernels, combine(): pl.pallas_call(combine_kernel, out_shape=jax.ShapeDtypeStruct((subspaces,...  36.3 us
    unnamed x9, local copies, waits for them, and re-layouts  3.97 us

profile of v2, /device:TPU:1, one launch (start us, length us, event | category | flops | bytes accessed | tf_op | source)
XLA Modules:
  0.0 144.0 jit_solution(16987400886214758931)
XLA Ops:
  0.6 0.0 copy-start
  0.6 1.6 %copy-done = bf16[8192,128]{1,0:T(8,128)(2,1)S(1)} copy-done((bf16[8192,128]{1,0:T(8,128)(2,1)S(1)}, bf16[8192,128]{1,0:T(8,128)(2,1)}, u32[]{:S(2)}) %copy-start) | copy-done | bytes 2097176
  2.2 0.0 copy-start.2
  2.2 0.8 copy-done.2
  3.0 0.0 copy-start.3
  3.0 0.7 copy-done.3
  3.6 0.0 copy-start.1
  3.6 47.7 %regroup_rows.1 = (bf16[8,1024,128]{2,1,0:T(8,128)(2,1)S(1)}, f32[8,128]{1,0:T(8,128)S(1)}) custom-call(bf16[8192,128]{1,0:T(8,128)(2,1)S(1)} %copy-done, s32[1,128]{1,0:T(1,128)S(1)} %bitcast.6, s32[8192]{0:T(1024)S(1)} %copy-done.2), custom_call_target="tpu_custom_call" | custom-call | tf_op jit(solution)/shard_map/regroup_rows/pallas_call | solution.py:277
  51.3 0.0 copy-done.1
  51.3 55.4 %assign_codes.1 = (bf16[1024,1024]{1,0:T(8,128)(2,1)}, f32[64,24,256]{2,1,0:T(8,128)S(1)}) custom-call(f32[8,128]{1,0:T(8,128)S(1)} %get-tuple-element.6.energy_ref, bf16[8,1024,128]{2,1,0:T(8,128)(2,1)S(1)} %get-tuple-element.7.x_ref, bf16[64,16,256]{2,1,0:T(8,128)(2,1)S(1)} %bitcast.4), custom_call_target="tpu_custom_call" | custom-call | tf_op jit(solution)/shard_map/assign_codes/pallas_call | solution.py:143
  106.7 36.3 %combine_sums.1 = f32[64,16,256]{2,1,0:T(8,128)S(1)} custom-call(f32[64,24,256]{2,1,0:T(8,128)S(1)} %get-tuple-element.9.sums_ref, bf16[64,16,256]{2,1,0:T(8,128)(2,1)S(1)} %bitcast.5), custom_call_target="tpu_custom_call" | custom-call | tf_op jit(solution)/shard_map/combine_sums/pallas_call | solution.py:395
  143.1 1.0 copy.7
Async XLA Ops:
  0.6 1.6 %copy-start = (bf16[8192,128]{1,0:T(8,128)(2,1)S(1)}, bf16[8192,128]{1,0:T(8,128)(2,1)}, u32[]{:S(2)}) copy-start(bf16[8192,128]{1,0:T(8,128)(2,1)} %emb_ref.1) | copy-start | bytes 6291460
  2.2 0.8 copy-start.2
  3.0 0.7 copy-start.3
  3.6 47.7 %copy-start.1 = (bf16[64,256,16]{1,2,0:T(8,128)(2,1)S(1)}, bf16[64,256,16]{1,2,0:T(8,128)(2,1)}, u32[]{:S(2)}) copy-start(bf16[64,256,16]{1,2,0:T(8,128)(2,1)} %param.7) | copy-start | bytes 1572868

commit v3 on v1

v3 whole, which is shorter than its diff:
```python
import math

import jax
import jax.numpy as jnp
from jax import lax
from jax.experimental import pallas as pl
from jax.experimental.pallas import tpu as pltpu
from jax.sharding import PartitionSpec as P

ANISO_GAIN = 1.0
SOFTNESS_LEVEL = 4.0
PRIOR_MASS = 1.0
STABILITY_FLOOR = 1e-06
LOG2E = math.log2(math.e)
NT = (((1,), (1,)), ((), ()))
F32 = jnp.float32
BF16 = jnp.bfloat16
LANES = 128


def hadamard(order):
    i = lax.broadcasted_iota(jnp.int32, (order, order), 0)
    j = lax.broadcasted_iota(jnp.int32, (order, order), 1)
    both = jnp.bitwise_and(i, j)
    parity = jnp.zeros((order, order), jnp.int32)
    for shift in range(order.bit_length() - 1):
        parity = parity + jnp.bitwise_and(jnp.right_shift(both, shift), 1)
    return (1 - 2 * jnp.bitwise_and(parity, 1)).astype(F32).astype(BF16)


def identity(order):
    i = lax.broadcasted_iota(jnp.int32, (order, order), 0)
    j = lax.broadcasted_iota(jnp.int32, (order, order), 1)
    return (i == j).astype(F32).astype(BF16)


def prepare_codes(m, ct_ref, c_ref, cb_ref, caug_ref):
    ct = ct_ref[m]
    width, codes = ct.shape
    wide = ct.astype(F32)
    c_ref[m] = wide.T.astype(BF16)
    square = jnp.sum(wide * wide, axis=0, keepdims=True) * (LOG2E / SOFTNESS_LEVEL)
    cb_ref[m] = jnp.broadcast_to(square, (LANES, codes)).T
    caug_ref[m, 0:width, :] = ct
    row = lax.broadcasted_iota(jnp.int32, (width, codes), 0)
    caug_ref[m, width : 2 * width, :] = jnp.where(row == 0, 1.0, 0.0).astype(BF16)


def rotate_block(block, rows, x_ref, rt_ref, own_ref, energy, width):
    outer = x_ref.shape[0]
    inner = x_ref.shape[2]
    h = hadamard(inner)
    parts = [
        lax.dot_general(h, x_ref[b, pl.ds(pl.multiple_of(block * rows, rows), rows), :], NT, preferred_element_type=F32)
        for b in range(outer)
    ]
    span = 1
    while span < outer:
        for b in range(outer):
            if not b & span:
                low, high = parts[b], parts[b | span]
                parts[b], parts[b | span] = low + high, low - high
        span *= 2
    scale = 1.0 / math.sqrt(outer * inner)
    total = jnp.zeros((1, rows), F32)
    for b in range(outer):
        rounded = (parts[b] * scale).astype(BF16)
        rt_ref[b * inner : (b + 1) * inner, :] = rounded
        wide = rounded.astype(F32)
        own = jnp.sum((wide * wide).reshape(inner // width, width, rows), axis=1)
        own_ref[b * (inner // width) : (b + 1) * (inner // width), :] = own
        total = total + jnp.sum(own, axis=0, keepdims=True)
    subspaces = outer * inner // width
    return ANISO_GAIN * subspaces * energy / (total * total + STABILITY_FLOOR)


def assign(ms, rows, stretch, rt_ref, own_ref, c_ref, cb_ref, caug_ref, dt_ref, sums_ref):
    width = c_ref.shape[2]
    ats = [pl.ds(pl.multiple_of(m * width, width), width) for m in ms]
    xs = [rt_ref[at, :] for at in ats]
    gs = [jnp.dot(c_ref[m], x, preferred_element_type=F32) for m, x in zip(ms, xs)]
    b = stretch * (LOG2E / SOFTNESS_LEVEL)
    es = []
    for m, g in zip(ms, gs):
        a = (1.0 + stretch * own_ref[pl.ds(m, 1), :]) * (2.0 * LOG2E / SOFTNESS_LEVEL)
        t = g * (a - b * g) - jnp.concatenate([cb_ref[m]] * (rows // LANES), axis=1)
        es.append(jnp.exp2(t - jnp.max(t, axis=0, keepdims=True)).astype(BF16))
    os = [jnp.dot(caug_ref[m], e, preferred_element_type=F32) for m, e in zip(ms, es)]
    row = lax.broadcasted_iota(jnp.int32, (width, rows), 0)
    lefts = []
    for at, o, x in zip(ats, os, xs):
        inv = 1.0 / o[width : width + 1, :]
        dt_ref[at, :] = (o[0:width, :] * inv).astype(BF16)
        inv_high = inv.astype(BF16).astype(F32)
        tail = jnp.where(row == 0, inv_high, jnp.where(row == 1, inv - inv_high, 0.0))
        lefts.append(jnp.concatenate([x.astype(F32) * inv, tail], axis=0).astype(BF16))
    ss = [lax.dot_general(left, e, NT, preferred_element_type=F32) for left, e in zip(lefts, es)]
    for m, s in zip(ms, ss):
        s = jnp.concatenate(
            [s[0:width], s[width : width + 1] + s[width + 1 : width + 2], s[width + 1 : width + 8]], axis=0
        )
        sums_ref[m] = sums_ref[m] + s


MESH = pl.DeviceIdType.MESH
GROUP = 8
SIDE = 4


def wait_bytes(ref, sem):
    pltpu.make_async_copy(ref, ref, sem).wait()


def remote(src, dst, there, send_sem, recv_sem):
    return pltpu.make_async_remote_copy(
        src_ref=src, dst_ref=dst, send_sem=send_sem, recv_sem=recv_sem, device_id=there, device_id_type=MESH
    )


def kernel(
    emb_hbm, sign_ref, order_hbm, ct_hbm, out_hbm, new_ref,
    emb_ref, order_ref, ct_ref, wide, send, x_ref,
    part, part_rows, got_dims, got_rows,
    c_ref, cb_ref, caug_ref, rt_ref, own_ref, dt_ref, dec_ref, sums_ref,
    low, counts, got_low, got_counts, both, got_both, piece_ref, all_ref,
    load_sem, emb_sem, send_sem, recv_sem, store_sem, esend_dims, erecv_dims, esend_rows, erecv_rows,
    sem_a, sem_b, sem_c, sem_d, sem_e, sem_f, sem_g, sem_h, sem_i, sem_j,
):
    r, d = lax.axis_index("rows"), lax.axis_index("dims")
    n_rows, n_dims = lax.axis_size("rows"), lax.axis_size("dims")
    devices, piece, inner = send.shape
    block = emb_ref.shape[0]
    subspaces, width, codes = ct_ref.shape
    outer, all_rows, _ = x_ref.shape
    rows = rt_ref.shape[1]
    blocks = all_rows // rows
    per_block = rows // piece
    chunks = emb_sem.shape[0]
    chunk = block // chunks

    order_load = pltpu.make_async_copy(order_hbm, order_ref, load_sem.at[0])
    ct_load = pltpu.make_async_copy(ct_hbm, ct_ref, load_sem.at[1])

    def emb_load(i):
        at = pl.ds(pl.multiple_of(i * chunk, chunk), chunk)
        return pltpu.make_async_copy(emb_hbm.at[at], emb_ref.at[at], emb_sem.at[i])

    for i in range(chunks):
        emb_load(i).start()
    order_load.start()
    ct_load.start()

    barrier = pltpu.get_barrier_semaphore()

    def greet(i, carry):
        there = lax.rem(r * n_dims + d + i, devices)
        pl.semaphore_signal(barrier, inc=1, device_id=(there // n_dims, lax.rem(there, n_dims)), device_id_type=MESH)
        return carry

    lax.fori_loop(1, devices, greet, 0)

    sign = sign_ref[...].astype(F32)

    def widen(i, acc):
        emb_load(i).wait()
        step = 256
        for h in range(chunk // step):
            at = pl.ds(pl.multiple_of(i * chunk + h * step, step), step)
            v = emb_ref[at, :].astype(F32)
            wide[at, :] = v * sign
            acc = acc + jnp.sum((v * v).reshape(step // 8, 8, inner), axis=0)
        return acc

    part[...] = lax.fori_loop(0, chunks, widen, jnp.zeros((8, inner), F32))
    order_load.wait()
    pl.semaphore_wait(barrier, devices - 1)

    for k in range(1, n_dims):
        there = (r, lax.rem(d + k, n_dims))
        remote(part, got_dims.at[k], there, esend_dims.at[k], erecv_dims.at[k]).start()

    def target(s, i, k):
        to_z = lax.rem(r // SIDE + i, SIDE)
        to_x = lax.rem(r + s + SIDE - i, SIDE)
        return to_z * SIDE + to_x, lax.rem(d + k + 2 * i, n_dims)

    def slot(s, i):
        return pl.ds(pl.multiple_of((s * per_block + i) * piece, piece), piece)

    def gather(s, i, k):
        to_r, to_d = target(s, i, k)
        q = to_r * n_dims + to_d
        first = q * piece
        for v in range(0, piece, 16):
            got = [wide[pl.ds(order_ref[first + v + u], 1), :] for u in range(16)]
            send[q, v : v + 16, :] = jnp.concatenate(got, axis=0).astype(BF16)
        return q, to_r, to_d

    def one_piece(s, i, k):
        q, to_r, to_d = gather(s, i, k)
        remote(send.at[q], x_ref.at[d, slot(s, i), :], (to_r, to_d), send_sem.at[s], recv_sem.at[s]).start()

    q, _, _ = gather(0, 0, 0)
    pltpu.make_async_copy(send.at[q], x_ref.at[d, slot(0, 0), :], recv_sem.at[0]).start()
    for i in range(1, per_block):
        one_piece(0, i, 0)

    def across(s, low_k):
        def step(k, carry):
            for i in range(per_block):
                one_piece(s, i, k)
            return carry

        lax.fori_loop(low_k, n_dims, step, 0)

    across(0, 1)
    total = part[...]
    for k in range(1, n_dims):
        wait_bytes(part, erecv_dims.at[k])
        total = total + got_dims[k]
    part_rows[...] = total
    for k in range(1, n_rows):
        there = (lax.rem(r + k, n_rows), d)
        remote(part_rows, got_rows.at[k], there, esend_rows.at[k], erecv_rows.at[k]).start()

    def later(s, carry):
        across(s, 0)
        return carry

    lax.fori_loop(1, blocks, later, 0)

    ct_load.wait()

    def prep(m, carry):
        prepare_codes(m, ct_ref, c_ref, cb_ref, caug_ref)
        sums_ref[m] = jnp.zeros(sums_ref.shape[1:], F32)
        return carry

    lax.fori_loop(0, subspaces, prep, 0)

    for k in range(1, n_rows):
        wait_bytes(part, erecv_rows.at[k])
        total = total + got_rows[k]
    energy = jnp.sum(total, keepdims=True) / (block * n_rows)

    def store(s, i):
        from_z = lax.rem(r // SIDE + SIDE - i, SIDE)
        from_x = lax.rem(r + 2 * SIDE - s + i, SIDE)
        at = pl.ds(pl.multiple_of((from_z * SIDE + from_x) * piece, piece), piece)
        return pltpu.make_async_copy(dec_ref.at[s, pl.ds(i * piece, piece), :], out_hbm.at[at, :], store_sem.at[s, i])

    def group_sums(k):
        there = lax.rem(d + k, n_dims)
        at = pl.ds(pl.multiple_of(there * GROUP, GROUP), GROUP)
        to = (r, there)
        return (
            remote(low.at[at], got_low.at[k], to, sem_a.at[k], sem_b.at[k]),
            remote(counts.at[at], got_counts.at[k], to, sem_c.at[k], sem_d.at[k]),
        )

    def one_block(s, carry):
        wait_bytes(x_ref.at[:, pl.ds(pl.multiple_of(s * rows, rows), rows), :], recv_sem.at[s])
        stretch = rotate_block(s, rows, x_ref, rt_ref, own_ref, energy, width)

        def one_group(k, carry):
            there = lax.rem(d + k, n_dims)
            ms = [there * GROUP + i for i in range(GROUP)]
            assign(ms, rows, stretch, rt_ref, own_ref, c_ref, cb_ref, caug_ref, dt_ref, sums_ref)

            @pl.when(jnp.logical_and(s == blocks - 1, k < n_dims))
            def _():
                for m in ms:
                    low[m] = sums_ref[m, 0:width, :].astype(BF16)
                    counts[pl.ds(m, 1), :] = sums_ref[m, width : width + 1, :]
                for copy in group_sums(k):
                    copy.start()

            return carry

        lax.fori_loop(1, n_dims + 1, one_group, 0)
        eye = identity(rows)
        for b in range(outer):
            lanes = slice(b * inner, (b + 1) * inner)
            flipped = lax.dot_general(eye, dt_ref[lanes, :], NT, preferred_element_type=F32)
            dec_ref[s, :, lanes] = flipped.astype(BF16)
        for i in range(per_block):
            store(s, i).start()
        return carry

    lax.fori_loop(0, blocks, one_block, 0)

    group = subspaces // n_dims
    half = codes * group // n_rows
    halves = codes // half
    sent = []

    def go(*args):
        copy = remote(*args)
        copy.start()
        sent.append(copy)

    mine = pl.ds(pl.multiple_of(d * group, group), group)
    total = sums_ref[mine, 0:width, :]
    total_counts = sums_ref[mine, width, :]
    for k in range(1, n_dims):
        wait_bytes(got_low.at[k], sem_b.at[k])
        wait_bytes(got_counts.at[k], sem_d.at[k])
        total = total + got_low[k].astype(F32)
        total_counts = total_counts + got_counts[k]
    for g in range(group):
        for h in range(halves):
            lanes = slice(h * half, (h + 1) * half)
            both[g * halves + h, 0:width, :] = total[g, :, lanes]
            both[g * halves + h, width : width + 8, :] = jnp.broadcast_to(total_counts[g : g + 1, lanes], (8, half))
    for k in range(1, n_rows):
        there = lax.rem(r + k, n_rows)
        go(both.at[there], got_both.at[k], (there, d), sem_e.at[k], sem_f.at[k])
    total = both[r]
    for k in range(1, n_rows):
        wait_bytes(got_both.at[k], sem_f.at[k])
        total = total + got_both[k]

    own_g = d * group + r // halves
    own_lanes = pl.ds(pl.multiple_of(lax.rem(r, halves) * half, half), half)
    new = (total[0:width] + PRIOR_MASS * ct_ref[own_g, :, own_lanes].astype(F32)) / (
        total[width : width + 1] + PRIOR_MASS
    )
    all_ref[d, r] = new
    for k in range(1, n_rows):
        there = lax.rem(r + k, n_rows)
        go(all_ref.at[d, r], all_ref.at[d, r], (there, d), sem_g.at[k], sem_h.at[k])
    for k in range(1, n_rows):
        wait_bytes(all_ref.at[d, lax.rem(r + n_rows - k, n_rows)], sem_h.at[k])
    for k in range(1, n_dims):
        go(all_ref.at[d], all_ref.at[d], (r, lax.rem(d + k, n_dims)), sem_i.at[k], sem_j.at[k])
    for k in range(1, n_dims):
        wait_bytes(all_ref.at[lax.rem(d + n_dims - k, n_dims)], sem_j.at[k])
    for e in range(n_dims):
        for g in range(group):
            for h in range(halves):
                new_ref[e * group + g, :, h * half : (h + 1) * half] = all_ref[e, g * halves + h].astype(F32)

    for copy in sent:
        copy.wait_send()
    for k in range(1, n_dims):
        for copy in group_sums(k):
            copy.wait_send()
        wait_bytes(part, esend_dims.at[k])
    for k in range(1, n_rows):
        wait_bytes(part, esend_rows.at[k])
    for s in range(blocks):
        wait_bytes(send.at[pl.ds(0, per_block * n_dims - (s == 0))], send_sem.at[s])
        for i in range(per_block):
            store(s, i).wait()


def body(embeddings, sign_flips, row_order, codebook):
    ct = codebook.transpose(0, 2, 1)
    n_rows, n_dims = lax.axis_size("rows"), lax.axis_size("dims")
    block, inner = embeddings.shape
    devices = n_rows * n_dims
    piece = block // devices
    subspaces, width, codes = ct.shape
    all_rows = block // n_dims
    rows = 256
    blocks = all_rows // rows
    group = subspaces // n_dims
    half = codes * group // n_rows
    full = n_dims * inner
    vmem = pl.BlockSpec(memory_space=pltpu.VMEM)
    hbm = pl.BlockSpec(memory_space=pl.ANY)
    dma = pltpu.SemaphoreType.DMA
    decoded, new = pl.pallas_call(
        kernel,
        out_shape=(
            jax.ShapeDtypeStruct((all_rows, full), BF16),
            jax.ShapeDtypeStruct((subspaces, width, codes), F32),
        ),
        in_specs=[hbm, vmem, hbm, hbm],
        out_specs=(hbm, vmem),
        scratch_shapes=[
            pltpu.VMEM((block, inner), BF16),
            pltpu.SMEM((block,), jnp.int32),
            pltpu.VMEM((subspaces, width, codes), BF16),
            pltpu.VMEM((block, inner), F32),
            pltpu.VMEM((devices, piece, inner), BF16),
            pltpu.VMEM((n_dims, all_rows, inner), BF16),
            pltpu.VMEM((8, inner), F32),
            pltpu.VMEM((8, inner), F32),
            pltpu.VMEM((n_dims, 8, inner), F32),
            pltpu.VMEM((n_rows, 8, inner), F32),
            pltpu.VMEM((subspaces, codes, width), BF16),
            pltpu.VMEM((subspaces, codes, LANES), F32),
            pltpu.VMEM((subspaces, 2 * width, codes), BF16),
            pltpu.VMEM((full, rows), BF16),
            pltpu.VMEM((subspaces, rows), F32),
            pltpu.VMEM((full, rows), BF16),
            pltpu.VMEM((blocks, rows, full), BF16),
            pltpu.VMEM((subspaces, width + 8, codes), F32),
            pltpu.VMEM((subspaces, width, codes), BF16),
            pltpu.VMEM((subspaces, codes), F32),
            pltpu.VMEM((n_dims, group, width, codes), BF16),
            pltpu.VMEM((n_dims, group, codes), F32),
            pltpu.VMEM((n_rows, width + 8, half), F32),
            pltpu.VMEM((n_rows, width + 8, half), F32),
            pltpu.VMEM((width, half), F32),
            pltpu.VMEM((n_dims, n_rows, width, half), F32),
            dma((2,)),
            dma((8,)),
            dma((blocks,)),
            dma((blocks,)),
            dma((blocks, rows // piece)),
        ]
        + [dma((n_dims,))] * 2
        + [dma((n_rows,))] * 2
        + [dma((n_dims,))] * 4
        + [dma((n_rows,))] * 4
        + [dma((n_dims,))] * 2,
        compiler_params=pltpu.CompilerParams(
            collective_id=0, has_side_effects=True, vmem_limit_bytes=56 * 1024 * 1024
        ),
        name="update_codes",
    )(embeddings, sign_flips.reshape(1, inner), row_order, ct)
    return decoded, new.transpose(0, 2, 1)


def solution(mesh):
    return jax.shard_map(
        body,
        mesh=mesh,
        in_specs=(P("rows", "dims"), P("dims"), P("rows"), P()),
        out_specs=(P(("rows", "dims"), None), P()),
        check_vma=False,
    )
```

time: 406 us -> 117 us (0.29)
  waiting for transfers between devices: 147 us -> 0 us
  blocking collectives: 79.6 us -> 0 us
  local copies, waits for them, and re-layouts: 31.4 us -> 4.14 us
  between operations: 14.7 us -> 0.65 us
  starting transfers between devices: 12 us -> 0 us
  other arithmetic: 8.32 us -> 0 us
    psum x1 -> x0, waiting for transfers between devices: 147 us -> none  [body(): sums = lax.psum(sums[:, :width + 1], ('rows', 'dims'))]
    psum x1 -> x0, blocking collectives: 79.6 us -> none  [body(): energy_total = lax.psum(jnp.sum(wide_input * wide_input), ('rows', 'dims'))]
    gather x1 -> x0, local copies, waits for them, and re-layouts: 29.5 us -> none  [body(): outgoing = signed[row_order].reshape(devices, piece_rows, local_width)]
    all_to_all x1 -> x0, starting transfers between devices: 12 us -> none  [body(): lax.all_to_all(outgoing, ('rows', 'dims'), split_axis=0, concat_axis=0, t...]
    unnamed x5 -> x4, local copies, waits for them, and re-layouts: 0.02 us -> 4.14 us
  transfers between devices with their start and end apart: 2 -> 0, of which waited for: 1 -> 0; matrix products, arithmetic and copies ran while one was open for 0% -> 0% of each run, Pallas kernels for 0% -> 0%
where the time goes in v3:
time: 117 us
  Pallas kernels  112 us (96%)
  local copies, waits for them, and re-layouts  4.14 us (4%)
    pallas_call x1, Pallas kernels, body(): pl.pallas_call(kernel, out_shape=(jax.ShapeDtypeStruct((all_rows, full),...  112 us
    unnamed x4, local copies, waits for them, and re-layouts  4.14 us

profile of v3, /device:TPU:1, one launch (start us, length us, event | category | flops | bytes accessed | tf_op | source)
XLA Modules:
  0.0 117.2 jit_solution(15141989594032587791)
XLA Ops:
  0.6 112.4 %update_codes.1 = (bf16[1024,1024]{1,0:T(8,128)(2,1)}, f32[64,16,256]{2,1,0:T(8,128)}) custom-call(bf16[8192,128]{1,0:T(8,128)(2,1)} %emb_hbm.1, s32[1,128]{1,0:T(1,128)} %bitcast.5, s32[8192]{0:T(1024)} %order_hbm.1, bf16[64,16,256]{2,1,0:T(8,128)(2,1)} %bitcast.4), custom_call_target="tpu_custom_call" | custom-call | tf_op jit(solution)/shard_map/update_codes/pallas_call | solution.py:373
  113.1 0.0 copy-start
  113.1 3.2 %copy.8 = bf16[1024,1024]{1,0:T(8,128)(2,1)} copy(bf16[1024,1024]{1,0:T(8,128)(2,1)} %get-tuple-element.8) | data formatting | bytes 4194304
  116.2 0.0 copy-done
  116.2 1.0 copy.9
Async XLA Ops:
  113.1 3.2 %copy-start = (f32[64,16,256]{2,1,0:T(8,128)S(1)}, f32[64,16,256]{2,1,0:T(8,128)}, u32[]{:S(2)}) copy-start(f32[64,16,256]{2,1,0:T(8,128)} %get-tuple-element.5) | copy-start | bytes 3145732

commit v4 on v3

--- a/solution.py
+++ b/solution.py
@@ -74,36 +74,45 @@
     return ANISO_GAIN * subspaces * energy / (total * total + STABILITY_FLOOR)
 
 
-def assign(ms, rows, stretch, rt_ref, own_ref, c_ref, cb_ref, caug_ref, dt_ref, sums_ref):
-    width = c_ref.shape[2]
-    ats = [pl.ds(pl.multiple_of(m * width, width), width) for m in ms]
-    xs = [rt_ref[at, :] for at in ats]
-    gs = [jnp.dot(c_ref[m], x, preferred_element_type=F32) for m, x in zip(ms, xs)]
+def score(m, k, rows, stretch, own_ref, rt_ref, c_ref, cb_ref, t_refs, top_refs):
+    codes, width = c_ref.shape[1:]
+    x = rt_ref[pl.ds(pl.multiple_of(m * width, width), width), :]
+    a = (1.0 + stretch * own_ref[pl.ds(m, 1), :]) * (2.0 * LOG2E / SOFTNESS_LEVEL)
     b = stretch * (LOG2E / SOFTNESS_LEVEL)
-    es = []
-    for m, g in zip(ms, gs):
-        a = (1.0 + stretch * own_ref[pl.ds(m, 1), :]) * (2.0 * LOG2E / SOFTNESS_LEVEL)
-        t = g * (a - b * g) - jnp.concatenate([cb_ref[m]] * (rows // LANES), axis=1)
-        es.append(jnp.exp2(t - jnp.max(t, axis=0, keepdims=True)).astype(BF16))
-    os = [jnp.dot(caug_ref[m], e, preferred_element_type=F32) for m, e in zip(ms, es)]
-    row = lax.broadcasted_iota(jnp.int32, (width, rows), 0)
-    lefts = []
-    for at, o, x in zip(ats, os, xs):
-        inv = 1.0 / o[width : width + 1, :]
-        dt_ref[at, :] = (o[0:width, :] * inv).astype(BF16)
-        inv_high = inv.astype(BF16).astype(F32)
-        tail = jnp.where(row == 0, inv_high, jnp.where(row == 1, inv - inv_high, 0.0))
-        lefts.append(jnp.concatenate([x.astype(F32) * inv, tail], axis=0).astype(BF16))
-    ss = [lax.dot_general(left, e, NT, preferred_element_type=F32) for left, e in zip(lefts, es)]
-    for m, s in zip(ms, ss):
-        s = jnp.concatenate(
-            [s[0:width], s[width : width + 1] + s[width + 1 : width + 2], s[width + 1 : width + 8]], axis=0
-        )
-        sums_ref[m] = sums_ref[m] + s
+    g = jnp.dot(c_ref[m], x, preferred_element_type=F32)
+    t = g * (a - b * g) - jnp.concatenate([cb_ref[m]] * (rows // LANES), axis=1)
+    t_refs[k % 2][...] = t
+    top_refs[k % 2][...] = jnp.max(t.reshape(codes // 8, 8, rows), axis=0)
+
+
+def raise_scores(k, t_refs, top_refs, e_refs):
+    top = jnp.max(top_refs[k % 2][...], axis=0, keepdims=True)
+    e_refs[k % 4][...] = jnp.exp2(t_refs[k % 2][...] - top).astype(BF16)
+
+
+def decode(m, k, rt_ref, caug_ref, dt_ref, e_refs, left_refs):
+    width = caug_ref.shape[1] // 2
+    at = pl.ds(pl.multiple_of(m * width, width), width)
+    o = jnp.dot(caug_ref[m], e_refs[k % 4][...], preferred_element_type=F32)
+    inv = 1.0 / o[width : width + 1, :]
+    dt_ref[at, :] = (o[0:width, :] * inv).astype(BF16)
+    row = lax.broadcasted_iota(jnp.int32, (width, o.shape[1]), 0)
+    high = inv.astype(BF16).astype(F32)
+    tail = jnp.where(row == 0, high, jnp.where(row == 1, inv - high, 0.0))
+    left_refs[k % 2][...] = jnp.concatenate([rt_ref[at, :].astype(F32) * inv, tail], axis=0).astype(BF16)
+
+
+def accumulate(m, k, sums_ref, e_refs, left_refs):
+    width = left_refs[0].shape[0] // 2
+    s = lax.dot_general(left_refs[k % 2][...], e_refs[k % 4][...], NT, preferred_element_type=F32)
+    s = jnp.concatenate(
+        [s[0:width], s[width : width + 1] + s[width + 1 : width + 2], s[width + 1 : width + 8]], axis=0
+    )
+    sums_ref[m] = sums_ref[m] + s
 
 
 MESH = pl.DeviceIdType.MESH
-GROUP = 8
+SPAN = 16
 SIDE = 4
 
 
@@ -118,12 +127,13 @@
 
 
 def kernel(
-    emb_hbm, sign_ref, order_hbm, ct_hbm, out_hbm, new_ref,
+    emb_hbm, sign_ref, order_hbm, ct_hbm, out_ref, new_ref,
     emb_ref, order_ref, ct_ref, wide, send, x_ref,
     part, part_rows, got_dims, got_rows,
-    c_ref, cb_ref, caug_ref, rt_ref, own_ref, dt_ref, dec_ref, sums_ref,
-    low, counts, got_low, got_counts, both, got_both, piece_ref, all_ref,
-    load_sem, emb_sem, send_sem, recv_sem, store_sem, esend_dims, erecv_dims, esend_rows, erecv_rows,
+    c_ref, cb_ref, caug_ref, rt_ref, own_ref, dt_ref, sums_ref,
+    t_0, t_1, e_0, e_1, e_2, e_3, left_0, left_1, top_0, top_1,
+    low, counts, got_low, got_counts, both, got_both, all_ref,
+    load_sem, emb_sem, send_sem, recv_sem, esend_dims, erecv_dims, esend_rows, erecv_rows,
     sem_a, sem_b, sem_c, sem_d, sem_e, sem_f, sem_g, sem_h, sem_i, sem_j,
 ):
     r, d = lax.axis_index("rows"), lax.axis_index("dims")
@@ -135,6 +145,9 @@
     rows = rt_ref.shape[1]
     blocks = all_rows // rows
     per_block = rows // piece
+    group = subspaces // n_dims
+    half = codes * group // n_rows
+    halves = codes // half
     chunks = emb_sem.shape[0]
     chunk = block // chunks
 
@@ -152,12 +165,14 @@
 
     barrier = pltpu.get_barrier_semaphore()
 
-    def greet(i, carry):
-        there = lax.rem(r * n_dims + d + i, devices)
-        pl.semaphore_signal(barrier, inc=1, device_id=(there // n_dims, lax.rem(there, n_dims)), device_id_type=MESH)
-        return carry
-
-    lax.fori_loop(1, devices, greet, 0)
+    def greet(j, low_k):
+        for k in range(low_k, n_dims):
+            there = (lax.rem(r + j, n_rows), lax.rem(d + k, n_dims))
+            pl.semaphore_signal(barrier, inc=1, device_id=there, device_id_type=MESH)
+        return low_k
+
+    greet(0, 1)
+    lax.fori_loop(1, n_rows, lambda j, carry: greet(j, 0) + carry, 0)
 
     sign = sign_ref[...].astype(F32)
 
@@ -173,11 +188,6 @@
 
     part[...] = lax.fori_loop(0, chunks, widen, jnp.zeros((8, inner), F32))
     order_load.wait()
-    pl.semaphore_wait(barrier, devices - 1)
-
-    for k in range(1, n_dims):
-        there = (r, lax.rem(d + k, n_dims))
-        remote(part, got_dims.at[k], there, esend_dims.at[k], erecv_dims.at[k]).start()
 
     def target(s, i, k):
         to_z = lax.rem(r // SIDE + i, SIDE)
@@ -194,26 +204,44 @@
         for v in range(0, piece, 16):
             got = [wide[pl.ds(order_ref[first + v + u], 1), :] for u in range(16)]
             send[q, v : v + 16, :] = jnp.concatenate(got, axis=0).astype(BF16)
-        return q, to_r, to_d
-
-    def one_piece(s, i, k):
-        q, to_r, to_d = gather(s, i, k)
+
+    def issue(s, i, k):
+        to_r, to_d = target(s, i, k)
+        q = to_r * n_dims + to_d
         remote(send.at[q], x_ref.at[d, slot(s, i), :], (to_r, to_d), send_sem.at[s], recv_sem.at[s]).start()
 
-    q, _, _ = gather(0, 0, 0)
-    pltpu.make_async_copy(send.at[q], x_ref.at[d, slot(0, 0), :], recv_sem.at[0]).start()
+    def across(s, low_k, *steps):
+        def step(k, carry):
+            for one in steps:
+                for i in range(per_block):
+                    one(s, i, k)
+            return carry
+
+        lax.fori_loop(low_k, n_dims, step, 0)
+
+    across(0, 0, gather)
+    across(1, 0, gather)
+    pl.semaphore_wait(barrier, devices - 1)
+
+    for k in range(1, n_dims):
+        there = (r, lax.rem(d + k, n_dims))
+        remote(part, got_dims.at[k], there, esend_dims.at[k], erecv_dims.at[k]).start()
+    pltpu.make_async_copy(send.at[r * n_dims + d], x_ref.at[d, slot(0, 0), :], recv_sem.at[0]).start()
     for i in range(1, per_block):
-        one_piece(0, i, 0)
-
-    def across(s, low_k):
-        def step(k, carry):
-            for i in range(per_block):
-                one_piece(s, i, k)
-            return carry
-
-        lax.fori_loop(low_k, n_dims, step, 0)
-
-    across(0, 1)
+        issue(0, i, 0)
+    across(0, 1, issue)
+
+    ct_load.wait()
+
+    def prep(i, carry):
+        for k in range(8):
+            prepare_codes(i * 8 + k, ct_ref, c_ref, cb_ref, caug_ref)
+            sums_ref[i * 8 + k] = jnp.zeros(sums_ref.shape[1:], F32)
+        return carry
+
+    lax.fori_loop(0, subspaces // 8, prep, 0)
+    across(1, 0, issue)
+
     total = part[...]
     for k in range(1, n_dims):
         wait_bytes(part, erecv_dims.at[k])
@@ -222,76 +250,100 @@
     for k in range(1, n_rows):
         there = (lax.rem(r + k, n_rows), d)
         remote(part_rows, got_rows.at[k], there, esend_rows.at[k], erecv_rows.at[k]).start()
-
-    def later(s, carry):
-        across(s, 0)
-        return carry
-
-    lax.fori_loop(1, blocks, later, 0)
-
-    ct_load.wait()
-
-    def prep(m, carry):
-        prepare_codes(m, ct_ref, c_ref, cb_ref, caug_ref)
-        sums_ref[m] = jnp.zeros(sums_ref.shape[1:], F32)
-        return carry
-
-    lax.fori_loop(0, subspaces, prep, 0)
-
+    across(2, 0, gather, issue)
     for k in range(1, n_rows):
         wait_bytes(part, erecv_rows.at[k])
         total = total + got_rows[k]
     energy = jnp.sum(total, keepdims=True) / (block * n_rows)
 
-    def store(s, i):
-        from_z = lax.rem(r // SIDE + SIDE - i, SIDE)
-        from_x = lax.rem(r + 2 * SIDE - s + i, SIDE)
-        at = pl.ds(pl.multiple_of((from_z * SIDE + from_x) * piece, piece), piece)
-        return pltpu.make_async_copy(dec_ref.at[s, pl.ds(i * piece, piece), :], out_hbm.at[at, :], store_sem.at[s, i])
+    cores = 2
+    ys = n_dims // cores
+    y, core = d // cores, lax.rem(d, cores)
+
+    def chunk_at(k):
+        return lax.rem(y + k // cores, ys) * cores + lax.rem(core + lax.rem(k, cores), cores)
 
     def group_sums(k):
-        there = lax.rem(d + k, n_dims)
-        at = pl.ds(pl.multiple_of(there * GROUP, GROUP), GROUP)
+        there = chunk_at(k)
+        at = pl.ds(pl.multiple_of(there * group, group), group)
         to = (r, there)
         return (
             remote(low.at[at], got_low.at[k], to, sem_a.at[k], sem_b.at[k]),
             remote(counts.at[at], got_counts.at[k], to, sem_c.at[k], sem_d.at[k]),
         )
 
-    def one_block(s, carry):
-        wait_bytes(x_ref.at[:, pl.ds(pl.multiple_of(s * rows, rows), rows), :], recv_sem.at[s])
-        stretch = rotate_block(s, rows, x_ref, rt_ref, own_ref, energy, width)
-
-        def one_group(k, carry):
-            there = lax.rem(d + k, n_dims)
-            ms = [there * GROUP + i for i in range(GROUP)]
-            assign(ms, rows, stretch, rt_ref, own_ref, c_ref, cb_ref, caug_ref, dt_ref, sums_ref)
-
-            @pl.when(jnp.logical_and(s == blocks - 1, k < n_dims))
-            def _():
-                for m in ms:
-                    low[m] = sums_ref[m, 0:width, :].astype(BF16)
-                    counts[pl.ds(m, 1), :] = sums_ref[m, width : width + 1, :]
-                for copy in group_sums(k):
-                    copy.start()
-
-            return carry
-
-        lax.fori_loop(1, n_dims + 1, one_group, 0)
+    def send_sums(k):
+        for g in range(group):
+            m = chunk_at(k) * group + g
+            low[m] = sums_ref[m, 0:width, :].astype(BF16)
+            counts[pl.ds(m, 1), :] = sums_ref[m, width : width + 1, :]
+        for copy in group_sums(k):
+            copy.start()
+
+    t_refs, e_refs = (t_0, t_1), (e_0, e_1, e_2, e_3)
+    left_refs, top_refs = (left_0, left_1), (top_0, top_1)
+    spans = subspaces // SPAN
+
+    def flip(s):
         eye = identity(rows)
         for b in range(outer):
             lanes = slice(b * inner, (b + 1) * inner)
-            flipped = lax.dot_general(eye, dt_ref[lanes, :], NT, preferred_element_type=F32)
-            dec_ref[s, :, lanes] = flipped.astype(BF16)
-        for i in range(per_block):
-            store(s, i).start()
+            flipped = lax.dot_general(eye, dt_ref[lanes, :], NT, preferred_element_type=F32).astype(BF16)
+            for i in range(per_block):
+                from_z = lax.rem(r // SIDE + SIDE - i, SIDE)
+                from_x = lax.rem(r + 2 * SIDE - s + i, SIDE)
+                at = pl.ds(pl.multiple_of((from_z * SIDE + from_x) * piece, piece), piece)
+                out_ref[at, lanes] = flipped[i * piece : (i + 1) * piece]
+
+    def one_block(s, carry):
+        @pl.when(s == 1)
+        def _():
+            across(3, 0, gather, issue)
+
+        wait_bytes(x_ref.at[:, pl.ds(pl.multiple_of(s * rows, rows), rows), :], recv_sem.at[s])
+        stretch = rotate_block(s, rows, x_ref, rt_ref, own_ref, energy, width)
+
+        def at_step(span, k):
+            ahead = k // SPAN
+            return lax.rem(y + 1 + span + ahead + spans, spans) * SPAN + k - ahead * SPAN
+
+        def start(span, k):
+            score(at_step(span, k), k, rows, stretch, own_ref, rt_ref, c_ref, cb_ref, t_refs, top_refs)
+
+        def one_span(span, carry):
+            for k in range(SPAN):
+                start(span, k + 1)
+                decode(at_step(span, k - 1), k - 1, rt_ref, caug_ref, dt_ref, e_refs, left_refs)
+                m = at_step(span, k - 2)
+                if k < 2:
+                    m = jnp.where(span == 0, subspaces, m)
+                accumulate(m, k - 2, sums_ref, e_refs, left_refs)
+                raise_scores(k, t_refs, top_refs, e_refs)
+
+            @pl.when(jnp.logical_and(s == blocks - 1, span > 0))
+            def _():
+                for c in range(cores):
+                    send_sums(span * cores + c)
+
+            return carry
+
+        start(0, 0)
+        lax.fori_loop(0, spans, one_span, 0)
+        last = at_step(spans - 1, SPAN - 1)
+        decode(last, SPAN - 1, rt_ref, caug_ref, dt_ref, e_refs, left_refs)
+        accumulate(last - 1, SPAN - 2, sums_ref, e_refs, left_refs)
+        accumulate(last, SPAN - 1, sums_ref, e_refs, left_refs)
+
+        @pl.when(s < blocks - 1)
+        def _():
+            flip(s)
+
         return carry
 
     lax.fori_loop(0, blocks, one_block, 0)
-
-    group = subspaces // n_dims
-    half = codes * group // n_rows
-    halves = codes // half
+    for k in range(1, cores):
+        send_sums(k)
+
     sent = []
 
     def go(*args):
@@ -315,6 +367,7 @@
     for k in range(1, n_rows):
         there = lax.rem(r + k, n_rows)
         go(both.at[there], got_both.at[k], (there, d), sem_e.at[k], sem_f.at[k])
+    flip(blocks - 1)
     total = both[r]
     for k in range(1, n_rows):
         wait_bytes(got_both.at[k], sem_f.at[k])
@@ -325,20 +378,32 @@
     new = (total[0:width] + PRIOR_MASS * ct_ref[own_g, :, own_lanes].astype(F32)) / (
         total[width : width + 1] + PRIOR_MASS
     )
-    all_ref[d, r] = new
+    all_ref[d, r] = new.astype(BF16)
     for k in range(1, n_rows):
         there = lax.rem(r + k, n_rows)
         go(all_ref.at[d, r], all_ref.at[d, r], (there, d), sem_g.at[k], sem_h.at[k])
     for k in range(1, n_rows):
         wait_bytes(all_ref.at[d, lax.rem(r + n_rows - k, n_rows)], sem_h.at[k])
-    for k in range(1, n_dims):
-        go(all_ref.at[d], all_ref.at[d], (r, lax.rem(d + k, n_dims)), sem_i.at[k], sem_j.at[k])
-    for k in range(1, n_dims):
-        wait_bytes(all_ref.at[lax.rem(d + n_dims - k, n_dims)], sem_j.at[k])
-    for e in range(n_dims):
+    partner = (r, y * cores + 1 - core)
+    for k in range(1, ys):
+        go(all_ref.at[d], all_ref.at[d], (r, lax.rem(y + k, ys) * cores + core), sem_i.at[k], sem_j.at[k])
+    go(all_ref.at[d], all_ref.at[d], partner, sem_i.at[ys], sem_j.at[ys])
+
+    def publish(e):
         for g in range(group):
             for h in range(halves):
                 new_ref[e * group + g, :, h * half : (h + 1) * half] = all_ref[e, g * halves + h].astype(F32)
+
+    publish(d)
+    for k in range(1, ys):
+        e = lax.rem(y + ys - k, ys) * cores + core
+        wait_bytes(all_ref.at[e], sem_j.at[k])
+        go(all_ref.at[e], all_ref.at[e], partner, sem_i.at[ys + k], sem_j.at[ys + k])
+        publish(e)
+    for k in range(ys):
+        e = lax.rem(y + ys - k, ys) * cores + 1 - core
+        wait_bytes(all_ref.at[e], sem_j.at[ys + k])
+        publish(e)
 
     for copy in sent:
         copy.wait_send()
@@ -350,8 +415,6 @@
         wait_bytes(part, esend_rows.at[k])
     for s in range(blocks):
         wait_bytes(send.at[pl.ds(0, per_block * n_dims - (s == 0))], send_sem.at[s])
-        for i in range(per_block):
-            store(s, i).wait()
 
 
 def body(embeddings, sign_flips, row_order, codebook):
@@ -373,11 +436,11 @@
     decoded, new = pl.pallas_call(
         kernel,
         out_shape=(
-            jax.ShapeDtypeStruct((all_rows, full), BF16),
-            jax.ShapeDtypeStruct((subspaces, width, codes), F32),
+            pltpu.VMEM((all_rows, full), BF16),
+            pltpu.VMEM((subspaces, width, codes), F32),
         ),
         in_specs=[hbm, vmem, hbm, hbm],
-        out_specs=(hbm, vmem),
+        out_specs=(vmem, vmem),
         scratch_shapes=[
             pltpu.VMEM((block, inner), BF16),
             pltpu.SMEM((block,), jnp.int32),
@@ -395,21 +458,24 @@
             pltpu.VMEM((full, rows), BF16),
             pltpu.VMEM((subspaces, rows), F32),
             pltpu.VMEM((full, rows), BF16),
-            pltpu.VMEM((blocks, rows, full), BF16),
-            pltpu.VMEM((subspaces, width + 8, codes), F32),
+            pltpu.VMEM((subspaces + 1, width + 8, codes), F32),
+        ]
+        + [pltpu.VMEM((codes, rows), F32)] * 2
+        + [pltpu.VMEM((codes, rows), BF16)] * 4
+        + [pltpu.VMEM((2 * width, rows), BF16)] * 2
+        + [pltpu.VMEM((8, rows), F32)] * 2
+        + [
             pltpu.VMEM((subspaces, width, codes), BF16),
             pltpu.VMEM((subspaces, codes), F32),
             pltpu.VMEM((n_dims, group, width, codes), BF16),
             pltpu.VMEM((n_dims, group, codes), F32),
             pltpu.VMEM((n_rows, width + 8, half), F32),
             pltpu.VMEM((n_rows, width + 8, half), F32),
-            pltpu.VMEM((width, half), F32),
-            pltpu.VMEM((n_dims, n_rows, width, half), F32),
+            pltpu.VMEM((n_dims, n_rows, width, half), BF16),
             dma((2,)),
             dma((8,)),
             dma((blocks,)),
             dma((blocks,)),
-            dma((blocks, rows // piece)),
         ]
         + [dma((n_dims,))] * 2
         + [dma((n_rows,))] * 2

time: 117 us -> 98.6 us (0.84)
  Pallas kernels: 112 us -> 95.6 us
  local copies, waits for them, and re-layouts: 4.14 us -> 2.29 us
    pallas_call x1, Pallas kernels: 112 us -> 95.6 us  [body(): pl.pallas_call(kernel, out_shape=(pltpu.VMEM((all_rows, full), BF16), plt...]
    unnamed x4 -> x2, local copies, waits for them, and re-layouts: 4.14 us -> 2.29 us
where the time goes in v4:
time: 98.6 us; the launch traced here: 98.5 us
  Pallas kernels  95.6 us (97%)
  local copies, waits for them, and re-layouts  2.29 us (2%)
    pallas_call x1, Pallas kernels, body(): pl.pallas_call(kernel, out_shape=(pltpu.VMEM((all_rows, full), BF16), plt...  95.6 us
    unnamed x2, local copies, waits for them, and re-layouts  2.29 us

profile of v4, /device:TPU:1, one launch (start us, length us, event | category | flops | bytes accessed | tf_op | source)
XLA Modules:
  0.0 98.5 jit_solution(17075952126729316720)
XLA Ops:
  0.6 95.6 %update_codes.1 = (bf16[1024,1024]{1,0:T(8,128)(2,1)S(1)}, f32[64,16,256]{2,1,0:T(8,128)S(1)}) custom-call(bf16[8192,128]{1,0:T(8,128)(2,1)} %emb_hbm.1, s32[1,128]{1,0:T(1,128)} %bitcast.5, s32[8192]{0:T(1024)} %order_hbm.1, bf16[64,16,256]{2,1,0:T(8,128)(2,1)} %bitcast.4), custom_call_target="tpu_custom_call" | custom-call | tf_op jit(solution)/shard_map/update_codes/pallas_call | solution.py:436
  96.2 1.3 %copy.8 = bf16[1024,1024]{1,0:T(8,128)(2,1)} copy(bf16[1024,1024]{1,0:T(8,128)(2,1)S(1)} %get-tuple-element.6) | data formatting | bytes 4194304
  97.5 1.0 copy.9

commit v5 on v4

--- a/solution.py
+++ b/solution.py
@@ -46,7 +46,7 @@
     caug_ref[m, width : 2 * width, :] = jnp.where(row == 0, 1.0, 0.0).astype(BF16)
 
 
-def rotate_block(block, rows, x_ref, rt_ref, own_ref, energy, width):
+def rotate_block(block, rows, x_ref, rt_ref, own_ref, width):
     outer = x_ref.shape[0]
     inner = x_ref.shape[2]
     h = hadamard(inner)
@@ -70,8 +70,7 @@
         own = jnp.sum((wide * wide).reshape(inner // width, width, rows), axis=1)
         own_ref[b * (inner // width) : (b + 1) * (inner // width), :] = own
         total = total + jnp.sum(own, axis=0, keepdims=True)
-    subspaces = outer * inner // width
-    return ANISO_GAIN * subspaces * energy / (total * total + STABILITY_FLOOR)
+    return total
 
 
 def score(m, k, rows, stretch, own_ref, rt_ref, c_ref, cb_ref, t_refs, top_refs):
@@ -129,7 +128,7 @@
 def kernel(
     emb_hbm, sign_ref, order_hbm, ct_hbm, out_ref, new_ref,
     emb_ref, order_ref, ct_ref, wide, send, x_ref,
-    part, part_rows, got_dims, got_rows,
+    part, part_rows, energy_ref, got_dims, got_rows,
     c_ref, cb_ref, caug_ref, rt_ref, own_ref, dt_ref, sums_ref,
     t_0, t_1, e_0, e_1, e_2, e_3, left_0, left_1, top_0, top_1,
     low, counts, got_low, got_counts, both, got_both, all_ref,
@@ -165,14 +164,17 @@
 
     barrier = pltpu.get_barrier_semaphore()
 
-    def greet(j, low_k):
-        for k in range(low_k, n_dims):
-            there = (lax.rem(r + j, n_rows), lax.rem(d + k, n_dims))
-            pl.semaphore_signal(barrier, inc=1, device_id=there, device_id_type=MESH)
-        return low_k
-
-    greet(0, 1)
-    lax.fori_loop(1, n_rows, lambda j, carry: greet(j, 0) + carry, 0)
+    to_dims = [lax.rem(d + k, n_dims) for k in range(n_dims)]
+    to_zs = [lax.rem(r // SIDE + i, SIDE) * SIDE for i in range(SIDE)]
+    to_xs = [lax.rem(r + i, SIDE) for i in range(SIDE)]
+
+    def hops(step):
+        return sum(min(i, SIDE - i) for i in (step[0], step[1], step[2] // 2))
+
+    steps = [(i, j, k) for i in range(SIDE) for j in range(SIDE) for k in range(n_dims)]
+    for i, j, k in sorted(steps, key=hops, reverse=True):
+        if i or j or k:
+            pl.semaphore_signal(barrier, inc=1, device_id=(to_zs[i] + to_xs[j], to_dims[k]), device_id_type=MESH)
 
     sign = sign_ref[...].astype(F32)
 
@@ -190,9 +192,10 @@
     order_load.wait()
 
     def target(s, i, k):
-        to_z = lax.rem(r // SIDE + i, SIDE)
-        to_x = lax.rem(r + s + SIDE - i, SIDE)
-        return to_z * SIDE + to_x, lax.rem(d + k + 2 * i, n_dims)
+        to_r = to_zs[i] + lax.rem(r + s + SIDE - i, SIDE)
+        if isinstance(k, int):
+            return to_r, to_dims[(k + 2 * i) % n_dims]
+        return to_r, lax.rem(d + k + 2 * i, n_dims)
 
     def slot(s, i):
         return pl.ds(pl.multiple_of((s * per_block + i) * piece, piece), piece)
@@ -210,37 +213,27 @@
         q = to_r * n_dims + to_d
         remote(send.at[q], x_ref.at[d, slot(s, i), :], (to_r, to_d), send_sem.at[s], recv_sem.at[s]).start()
 
-    def across(s, low_k, *steps):
+    def gather_block(s):
         def step(k, carry):
-            for one in steps:
-                for i in range(per_block):
-                    one(s, i, k)
+            for i in range(per_block):
+                gather(s, i, k)
             return carry
 
-        lax.fori_loop(low_k, n_dims, step, 0)
-
-    across(0, 0, gather)
-    across(1, 0, gather)
+        lax.fori_loop(0, n_dims, step, 0)
+
+    def issue_block(s, first, last):
+        for n in range(first, last):
+            issue(s, n % per_block, n // per_block)
+
+    for b in range(blocks):
+        gather_block(b)
     pl.semaphore_wait(barrier, devices - 1)
 
     for k in range(1, n_dims):
-        there = (r, lax.rem(d + k, n_dims))
+        there = (r, to_dims[k])
         remote(part, got_dims.at[k], there, esend_dims.at[k], erecv_dims.at[k]).start()
     pltpu.make_async_copy(send.at[r * n_dims + d], x_ref.at[d, slot(0, 0), :], recv_sem.at[0]).start()
-    for i in range(1, per_block):
-        issue(0, i, 0)
-    across(0, 1, issue)
-
-    ct_load.wait()
-
-    def prep(i, carry):
-        for k in range(8):
-            prepare_codes(i * 8 + k, ct_ref, c_ref, cb_ref, caug_ref)
-            sums_ref[i * 8 + k] = jnp.zeros(sums_ref.shape[1:], F32)
-        return carry
-
-    lax.fori_loop(0, subspaces // 8, prep, 0)
-    across(1, 0, issue)
+    issue_block(0, 1, n_dims * per_block)
 
     total = part[...]
     for k in range(1, n_dims):
@@ -250,11 +243,17 @@
     for k in range(1, n_rows):
         there = (lax.rem(r + k, n_rows), d)
         remote(part_rows, got_rows.at[k], there, esend_rows.at[k], erecv_rows.at[k]).start()
-    across(2, 0, gather, issue)
-    for k in range(1, n_rows):
-        wait_bytes(part, erecv_rows.at[k])
-        total = total + got_rows[k]
-    energy = jnp.sum(total, keepdims=True) / (block * n_rows)
+    ct_load.wait()
+
+    def prep(i, carry):
+        for k in range(8):
+            prepare_codes(i * 8 + k, ct_ref, c_ref, cb_ref, caug_ref)
+            sums_ref[i * 8 + k] = jnp.zeros(sums_ref.shape[1:], F32)
+        return carry
+
+    lax.fori_loop(0, subspaces // 8, prep, 0)
+    wait_bytes(send.at[pl.ds(0, per_block * n_dims - 1)], send_sem.at[0])
+    issue_block(1, 0, n_dims * per_block)
 
     cores = 2
     ys = n_dims // cores
@@ -296,12 +295,18 @@
                 out_ref[at, lanes] = flipped[i * piece : (i + 1) * piece]
 
     def one_block(s, carry):
-        @pl.when(s == 1)
+        wait_bytes(x_ref.at[:, pl.ds(pl.multiple_of(s * rows, rows), rows), :], recv_sem.at[s])
+        norms = rotate_block(s, rows, x_ref, rt_ref, own_ref, width)
+
+        @pl.when(s == 0)
         def _():
-            across(3, 0, gather, issue)
-
-        wait_bytes(x_ref.at[:, pl.ds(pl.multiple_of(s * rows, rows), rows), :], recv_sem.at[s])
-        stretch = rotate_block(s, rows, x_ref, rt_ref, own_ref, energy, width)
+            total = part_rows[...]
+            for k in range(1, n_rows):
+                wait_bytes(part, erecv_rows.at[k])
+                total = total + got_rows[k]
+            energy_ref[...] = jnp.broadcast_to(jnp.sum(total, keepdims=True) / (block * n_rows), energy_ref.shape)
+
+        stretch = ANISO_GAIN * subspaces * energy_ref[0:1, 0:1] / (norms * norms + STABILITY_FLOOR)
 
         def at_step(span, k):
             ahead = k // SPAN
@@ -319,6 +324,14 @@
                     m = jnp.where(span == 0, subspaces, m)
                 accumulate(m, k - 2, sums_ref, e_refs, left_refs)
                 raise_scores(k, t_refs, top_refs, e_refs)
+
+            for late in range(2, blocks):
+                for half_block in range(2):
+
+                    @pl.when(jnp.logical_and(s == 0, span == (late - 2) * 2 + half_block))
+                    def _():
+                        count = n_dims * per_block // 2
+                        issue_block(late, half_block * count, (half_block + 1) * count)
 
             @pl.when(jnp.logical_and(s == blocks - 1, span > 0))
             def _():
@@ -413,8 +426,8 @@
         wait_bytes(part, esend_dims.at[k])
     for k in range(1, n_rows):
         wait_bytes(part, esend_rows.at[k])
-    for s in range(blocks):
-        wait_bytes(send.at[pl.ds(0, per_block * n_dims - (s == 0))], send_sem.at[s])
+    for s in range(1, blocks):
+        wait_bytes(send.at[pl.ds(0, per_block * n_dims)], send_sem.at[s])
 
 
 def body(embeddings, sign_flips, row_order, codebook):
@@ -448,6 +461,7 @@
             pltpu.VMEM((block, inner), F32),
             pltpu.VMEM((devices, piece, inner), BF16),
             pltpu.VMEM((n_dims, all_rows, inner), BF16),
+            pltpu.VMEM((8, inner), F32),
             pltpu.VMEM((8, inner), F32),
             pltpu.VMEM((8, inner), F32),
             pltpu.VMEM((n_dims, 8, inner), F32),

time: 98.6 us -> 91.9 us (0.932)
  Pallas kernels: 95.6 us -> 88.9 us
    pallas_call x1, Pallas kernels: 95.6 us -> 88.9 us  [body(): pl.pallas_call(kernel, out_shape=(pltpu.VMEM((all_rows, full), BF16), plt...]
where the time goes in v5:
time: 91.9 us; the launch traced here: 91.8 us
  Pallas kernels  88.9 us (97%)
  local copies, waits for them, and re-layouts  2.29 us (2%)
    pallas_call x1, Pallas kernels, body(): pl.pallas_call(kernel, out_shape=(pltpu.VMEM((all_rows, full), BF16), plt...  88.9 us
    unnamed x2, local copies, waits for them, and re-layouts  2.29 us

profile of v5, /device:TPU:1, one launch (start us, length us, event | category | flops | bytes accessed | tf_op | source)
XLA Modules:
  0.0 91.8 jit_solution(5905349771411724188)
XLA Ops:
  0.6 88.9 %update_codes.1 = (bf16[1024,1024]{1,0:T(8,128)(2,1)S(1)}, f32[64,16,256]{2,1,0:T(8,128)S(1)}) custom-call(bf16[8192,128]{1,0:T(8,128)(2,1)} %emb_hbm.1, s32[1,128]{1,0:T(1,128)} %bitcast.5, s32[8192]{0:T(1024)} %order_hbm.1, bf16[64,16,256]{2,1,0:T(8,128)(2,1)} %bitcast.4), custom_call_target="tpu_custom_call" | custom-call | tf_op jit(solution)/shard_map/update_codes/pallas_call | solution.py:449
  89.5 1.3 %copy.8 = bf16[1024,1024]{1,0:T(8,128)(2,1)} copy(bf16[1024,1024]{1,0:T(8,128)(2,1)S(1)} %get-tuple-element.6) | data formatting | bytes 4194304
  90.8 1.0 %copy.9 = f32[64,256,16]{1,2,0:T(8,128)} copy(f32[64,256,16]{1,2,0:T(8,128)S(1)} %bitcast.3) | data formatting | bytes 2097152

commit v6 on v5

--- a/solution.py
+++ b/solution.py
@@ -279,6 +279,11 @@
         for copy in group_sums(k):
             copy.start()
 
+    def turn(span, h):
+        dy = jnp.where(span == 0, 2, jnp.where(span == spans - 1, 0, 1 + 2 * h))
+        dcore = jnp.where(span == 0, h, jnp.where(span == spans - 1, 1 - h, span - 1))
+        return dy * cores + dcore
+
     t_refs, e_refs = (t_0, t_1), (e_0, e_1, e_2, e_3)
     left_refs, top_refs = (left_0, left_1), (top_0, top_1)
     spans = subspaces // SPAN
@@ -309,11 +314,17 @@
         stretch = ANISO_GAIN * subspaces * energy_ref[0:1, 0:1] / (norms * norms + STABILITY_FLOOR)
 
         def at_step(span, k):
-            ahead = k // SPAN
-            return lax.rem(y + 1 + span + ahead + spans, spans) * SPAN + k - ahead * SPAN
+            ahead, k = k // SPAN, k % SPAN
+            return chunk_at(turn(lax.rem(span + ahead + spans, spans), k // group)) * group + k % group
 
         def start(span, k):
             score(at_step(span, k), k, rows, stretch, own_ref, rt_ref, c_ref, cb_ref, t_refs, top_refs)
+
+        def drain(span):
+            last = at_step(span, SPAN - 1)
+            decode(last, SPAN - 1, rt_ref, caug_ref, dt_ref, e_refs, left_refs)
+            accumulate(last - 1, SPAN - 2, sums_ref, e_refs, left_refs)
+            accumulate(last, SPAN - 1, sums_ref, e_refs, left_refs)
 
         def one_span(span, carry):
             for k in range(SPAN):
@@ -321,7 +332,7 @@
                 decode(at_step(span, k - 1), k - 1, rt_ref, caug_ref, dt_ref, e_refs, left_refs)
                 m = at_step(span, k - 2)
                 if k < 2:
-                    m = jnp.where(span == 0, subspaces, m)
+                    m = jnp.where(jnp.logical_or(span == 0, s == blocks - 1), subspaces, m)
                 accumulate(m, k - 2, sums_ref, e_refs, left_refs)
                 raise_scores(k, t_refs, top_refs, e_refs)
 
@@ -333,22 +344,23 @@
                         count = n_dims * per_block // 2
                         issue_block(late, half_block * count, (half_block + 1) * count)
 
-            @pl.when(jnp.logical_and(s == blocks - 1, span > 0))
+            @pl.when(s == blocks - 1)
             def _():
-                for c in range(cores):
-                    send_sums(span * cores + c)
+                drain(span)
+
+                @pl.when(span < spans - 1)
+                def _():
+                    for h in range(SPAN // group):
+                        send_sums(turn(span, h))
 
             return carry
 
         start(0, 0)
         lax.fori_loop(0, spans, one_span, 0)
-        last = at_step(spans - 1, SPAN - 1)
-        decode(last, SPAN - 1, rt_ref, caug_ref, dt_ref, e_refs, left_refs)
-        accumulate(last - 1, SPAN - 2, sums_ref, e_refs, left_refs)
-        accumulate(last, SPAN - 1, sums_ref, e_refs, left_refs)
 
         @pl.when(s < blocks - 1)
         def _():
+            drain(spans - 1)
             flip(s)
 
         return carry

time: 91.9 us -> 89.7 us (0.976)
  Pallas kernels: 88.9 us -> 86.6 us
    pallas_call x1, Pallas kernels: 88.9 us -> 86.6 us  [body(): pl.pallas_call(kernel, out_shape=(pltpu.VMEM((all_rows, full), BF16), plt...]
where the time goes in v6:
time: 89.7 us; the launch traced here: 89.6 us
  Pallas kernels  86.6 us (97%)
  local copies, waits for them, and re-layouts  2.29 us (3%)
    pallas_call x1, Pallas kernels, body(): pl.pallas_call(kernel, out_shape=(pltpu.VMEM((all_rows, full), BF16), plt...  86.6 us
    unnamed x2, local copies, waits for them, and re-layouts  2.29 us

profile of v6, /device:TPU:1, one launch (start us, length us, event | category | flops | bytes accessed | tf_op | source)
XLA Modules:
  0.0 89.6 jit_solution(155184523903280503)
XLA Ops:
  0.6 86.6 %update_codes.1 = (bf16[1024,1024]{1,0:T(8,128)(2,1)S(1)}, f32[64,16,256]{2,1,0:T(8,128)S(1)}) custom-call(bf16[8192,128]{1,0:T(8,128)(2,1)} %emb_hbm.1, s32[1,128]{1,0:T(1,128)} %bitcast.5, s32[8192]{0:T(1024)} %order_hbm.1, bf16[64,16,256]{2,1,0:T(8,128)(2,1)} %bitcast.4), custom_call_target="tpu_custom_call" | custom-call | tf_op jit(solution)/shard_map/update_codes/pallas_call | solution.py:461
  87.3 1.3 %copy.8 = bf16[1024,1024]{1,0:T(8,128)(2,1)} copy(bf16[1024,1024]{1,0:T(8,128)(2,1)S(1)} %get-tuple-element.6) | data formatting | bytes 4194304
  88.6 1.0 %copy.9 = f32[64,256,16]{1,2,0:T(8,128)} copy(f32[64,256,16]{1,2,0:T(8,128)S(1)} %bitcast.3) | data formatting | bytes 2097152

commit v7 on v6

--- a/solution.py
+++ b/solution.py
@@ -410,7 +410,7 @@
     for k in range(1, n_rows):
         wait_bytes(all_ref.at[d, lax.rem(r + n_rows - k, n_rows)], sem_h.at[k])
     partner = (r, y * cores + 1 - core)
-    for k in range(1, ys):
+    for k in (2, 1, 3):
         go(all_ref.at[d], all_ref.at[d], (r, lax.rem(y + k, ys) * cores + core), sem_i.at[k], sem_j.at[k])
     go(all_ref.at[d], all_ref.at[d], partner, sem_i.at[ys], sem_j.at[ys])
 
@@ -420,13 +420,16 @@
                 new_ref[e * group + g, :, h * half : (h + 1) * half] = all_ref[e, g * halves + h].astype(F32)
 
     publish(d)
-    for k in range(1, ys):
+    for k in (1, 3, 2):
         e = lax.rem(y + ys - k, ys) * cores + core
         wait_bytes(all_ref.at[e], sem_j.at[k])
         go(all_ref.at[e], all_ref.at[e], partner, sem_i.at[ys + k], sem_j.at[ys + k])
-        publish(e)
-    for k in range(ys):
+        if k != 2:
+            publish(e)
+    for k in (0, 1, 3, 2):
         e = lax.rem(y + ys - k, ys) * cores + 1 - core
+        if k == 0:
+            publish(lax.rem(y + ys - 2, ys) * cores + core)
         wait_bytes(all_ref.at[e], sem_j.at[ys + k])
         publish(e)
 

time: 89.7 us -> 89 us (level)
  no operation moved by 1% of the time
where the time goes in v7:
time: 89 us; the launch traced here: 88.9 us
  Pallas kernels  86 us (97%)
  local copies, waits for them, and re-layouts  2.29 us (3%)
    pallas_call x1, Pallas kernels, body(): pl.pallas_call(kernel, out_shape=(pltpu.VMEM((all_rows, full), BF16), plt...  86 us
    unnamed x2, local copies, waits for them, and re-layouts  2.29 us

profile of v7, /device:TPU:1, one launch (start us, length us, event | category | flops | bytes accessed | tf_op | source)
XLA Modules:
  0.0 88.9 jit_solution(559138026035836491)
XLA Ops:
  0.6 86.0 %update_codes.1 = (bf16[1024,1024]{1,0:T(8,128)(2,1)S(1)}, f32[64,16,256]{2,1,0:T(8,128)S(1)}) custom-call(bf16[8192,128]{1,0:T(8,128)(2,1)} %emb_hbm.1, s32[1,128]{1,0:T(1,128)} %bitcast.5, s32[8192]{0:T(1024)} %order_hbm.1, bf16[64,16,256]{2,1,0:T(8,128)(2,1)} %bitcast.4), custom_call_target="tpu_custom_call" | custom-call | tf_op jit(solution)/shard_map/update_codes/pallas_call | solution.py:464
  86.6 1.3 %copy.8 = bf16[1024,1024]{1,0:T(8,128)(2,1)} copy(bf16[1024,1024]{1,0:T(8,128)(2,1)S(1)} %get-tuple-element.6) | data formatting | bytes 4194304
  87.9 1.0 %copy.9 = f32[64,256,16]{1,2,0:T(8,128)} copy(f32[64,256,16]{1,2,0:T(8,128)S(1)} %bitcast.3) | data formatting | bytes 2097152
